TPU v7x, 32 devices: a whole 2x2x4 slice. The times are simulated.
32 devices in a mesh: group: 2 (over x), tm: 16 (over z, y, core).
Axes of the slice: x: 2, y: 2, z: 4, core: 2. Of those that a mesh axis runs over, the one named last changes fastest.
Arguments:
- iterate: float32 [64, 2, 2, 96, 192], P(('group', 'tm')), parts along dimension 0, may hold values from 0 to 1
- labels: int32 [4, 96, 192], P('group'), parts along dimension 0, may hold values from 0 to 3
- stim_mask: int32 [4, 96, 192], P('group'), parts along dimension 0, may hold values 0 or 1
Outputs:
- corrected: float32 [64, 2, 2, 96, 192], P(('group', 'tm')), parts along dimension 0
There are 2 independent parts, one for each index of `group`. A program takes and returns all parts, laid end to end along the dimension named above; each array names one. Nothing has to cross between parts.
All inputs are finite; a program needn't handle non-finite values.
Results may differ from a plain program's by a relative error of at most 0.0003.
Values sent between devices are 32-bit elements; how exact they have to be, the bound alone decides.
A program may use at most 256 MiB of HBM per device.

v0:
```python
import jax
import jax.numpy as jnp
from jax import lax
from jax.sharding import PartitionSpec as P

MSTEPS = 8
PULSE = 16


time_step = 0.05
excite_gain = 8.0
threshold = 0.15
recovery_base = 0.005
recovery_gain = 0.2
recovery_shift = 0.3
pulse_height = 1.0
coarse_floor = -0.5
conduct_table = (0.1, 0.35, 0.7, 1.0)


def from_behind(value, axis, steps):
    count = lax.axis_size(axis)
    pairs = [(source, (source + steps) % count) for source in range(count)]
    return lax.ppermute(value, axis, pairs)


def prefix(value, axis, combine, identity):
    size, here = (lax.axis_size(axis), lax.axis_index(axis))
    everything = jax.tree.map(lambda part: lax.all_gather(part, axis), value)
    start = jax.tree.map(
        lambda part, zero: jnp.broadcast_to(jnp.asarray(zero, part.dtype), part.shape),
        value,
        identity,
    )

    def lap(k, before):
        reached = k < here
        new = combine(before, jax.tree.map(lambda part: part[k], everything))
        return jax.tree.map(lambda a, b: jnp.where(reached, a, b), new, before)

    return lax.fori_loop(0, size, lap, start)


def broadcast(value, axis, source):
    kept = jnp.where(lax.axis_index(axis) == source, value, 0).astype(value.dtype)
    return lax.psum(kept, axis)


def face_terms(labels):
    conduct = jnp.zeros(labels.shape, jnp.float32)
    for label_id, conduct_value in enumerate(conduct_table):
        conduct = conduct + jnp.where(
            labels == label_id, jnp.float32(conduct_value), jnp.float32(0.0)
        )
    along_x = 0.5 * (conduct[1:] + conduct[:-1])
    along_y = 0.5 * (conduct[:, 1:] + conduct[:, :-1])
    along_z = 0.5 * (conduct[:, :, 1:] + conduct[:, :, :-1])
    return (along_x, along_y, along_z)


def diffuse(potential, face_coeffs):
    along_x, along_y, along_z = face_coeffs
    face_flux = along_x * (potential[1:] - potential[:-1])
    result = jnp.pad(face_flux, ((0, 1), (0, 0), (0, 0))) - jnp.pad(
        face_flux, ((1, 0), (0, 0), (0, 0))
    )
    face_flux = along_y * (potential[:, 1:] - potential[:, :-1])
    result = (
        result
        + jnp.pad(face_flux, ((0, 0), (0, 1), (0, 0)))
        - jnp.pad(face_flux, ((0, 0), (1, 0), (0, 0)))
    )
    face_flux = along_z * (potential[:, :, 1:] - potential[:, :, :-1])
    result = (
        result
        + jnp.pad(face_flux, ((0, 0), (0, 0), (0, 1)))
        - jnp.pad(face_flux, ((0, 0), (0, 0), (1, 0)))
    )
    return result


def recovery_rate(potential, recovery):
    return recovery_base + recovery_gain * jnp.maximum(recovery, 0.0) / (
        jnp.maximum(potential, 0.0) + recovery_shift
    )


def fine_update(potential, recovery, face_coeffs, stimulus, switch):
    recover_rate = recovery_rate(potential, recovery)
    source = diffuse(potential, face_coeffs) - excite_gain * potential * (potential - threshold) * (
        potential - 1.0
    )
    source = source - potential * recovery + switch * stimulus
    new_potential = potential + time_step * source
    new_recovery = recovery + time_step * recover_rate * (
        -recovery - excite_gain * potential * (potential - threshold - 1.0)
    )
    return (new_potential, new_recovery)


def advance(c_state, face_coeffs, stimulus, first_step, beat_steps):

    def one_step(offset, running):
        moment = (first_step + offset) % beat_steps
        switch = jnp.where(moment < PULSE, 1.0, 0.0).astype(jnp.float32)
        return fine_update(running[0], running[1], face_coeffs, stimulus, switch)

    potential, recovery = lax.fori_loop(0, MSTEPS, one_step, (c_state[0], c_state[1]))
    return jnp.stack([potential, recovery])


def coarse_map(previous, relaxed):
    potential = jnp.clip(previous[0], 0.0, 1.0)
    recovery = jnp.maximum(previous[1], 0.0)
    recover_rate = recovery_rate(potential, recovery)
    horizon = MSTEPS * time_step
    fast_slope = jnp.minimum(
        -excite_gain
        * (3.0 * potential * potential - 2.0 * (1.0 + threshold) * potential + threshold)
        - recovery,
        coarse_floor,
    )
    cross_term = -recover_rate * excite_gain * (2.0 * potential - threshold - 1.0)
    first_diag = 1.0 / (1.0 - horizon * fast_slope)
    second_diag = 1.0 / (1.0 + horizon * recover_rate)
    lower_term = horizon * cross_term * first_diag * second_diag
    residual = previous - relaxed
    return (first_diag, lower_term, second_diag, residual[0], residual[1])


def compose(earlier, latter):
    return (
        latter[0] * earlier[0],
        latter[1] * earlier[0] + latter[2] * earlier[1],
        latter[2] * earlier[2],
        latter[0] * earlier[3] + latter[3],
        latter[1] * earlier[3] + latter[2] * earlier[4] + latter[4],
    )


def apply_map(mapping, first_in, second_in):
    return (
        mapping[0] * first_in + mapping[3],
        mapping[1] * first_in + mapping[2] * second_in + mapping[4],
    )


def loop_point(loop_map):
    first_part = loop_map[3] / (1.0 - loop_map[0])
    second = (loop_map[4] + loop_map[1] * first_part) / (1.0 - loop_map[2])
    return (first_part, second)


def on_device(iterate, labels, stim_mask):
    loop_size = lax.axis_size("tm")
    slot_count = iterate.shape[0]
    first_slice = lax.axis_index("tm") * slot_count
    beat_steps = loop_size * slot_count * MSTEPS
    face_coeffs = face_terms(labels)
    stimulus = pulse_height * stim_mask.astype(jnp.float32)
    predicted = [
        advance(iterate[offset], face_coeffs, stimulus, (first_slice + offset) * MSTEPS, beat_steps)
        for offset in range(slot_count)
    ]
    incoming = from_behind(predicted[-1], "tm", 1)
    relaxed = [incoming] + predicted[:-1]
    propagated = [
        advance(relaxed[offset], face_coeffs, stimulus, (first_slice + offset) * MSTEPS, beat_steps)
        for offset in range(slot_count)
    ]
    arrived = from_behind(propagated[-1], "tm", 1)
    previous = [arrived] + propagated[:-1]
    slot_maps = [coarse_map(previous[offset], relaxed[offset]) for offset in range(slot_count)]
    own_map = slot_maps[0]
    for mapping in slot_maps[1:]:
        own_map = compose(own_map, mapping)
    ones_field = jnp.ones(labels.shape, jnp.float32)
    zero_field = jnp.zeros(labels.shape, jnp.float32)
    identity = (ones_field, zero_field, ones_field, zero_field, zero_field)
    before = prefix(own_map, "tm", compose, identity)
    loop_map = jax.tree.map(
        lambda part: broadcast(part, "tm", loop_size - 1), compose(before, own_map)
    )
    loop_state = loop_point(loop_map)
    correction = apply_map(before, loop_state[0], loop_state[1])
    results = []
    for offset in range(slot_count):
        correction = apply_map(slot_maps[offset], correction[0], correction[1])
        results.append(relaxed[offset] + jnp.stack(correction))
    return jnp.stack(results)


def solution(mesh):
    in_specs = (
        P(("group", "tm"), None, None, None, None),
        P("group", None, None),
        P("group", None, None),
    )
    out_specs = P(("group", "tm"), None, None, None, None)
    return jax.shard_map(
        on_device, mesh=mesh, in_specs=in_specs, out_specs=out_specs, check_vma=False
    )
```

profile of v0, /device:TPU:0, one launch (start us, length us, event | category | flops | bytes accessed | tf_op | source)
XLA Modules:
  0.0 394.4 jit_solution(15376241448395824526)
XLA Ops:
  9.1 3.9 while.102
  13.6 3.9 while.103
  17.5 3.9 while.104
  21.5 2.7 collective-permute-start.1
  24.2 3.9 while.105
  28.2 3.8 collective-permute-done.1
  37.0 41.6 %all-gather.11.cloned.1.call-done = f32[32,96,192]{2,1,0:T(8,128)} async-done(((f32[2,96,192]{2,1,0:T(8,128)}), f32[32,96,192]{2,1,0:T(8,128)}) %all-gather.11.cloned.1.call-update) | async-done | bytes 2359312 | tf_op jit(solution)/shard_map/all_gather | solution.py:29
  78.6 46.3 %all-gather.17.cloned.1.call-done = f32[32,96,192]{2,1,0:T(8,128)} async-done(((f32[2,96,192]{2,1,0:T(8,128)}), f32[32,96,192]{2,1,0:T(8,128)}) %all-gather.17.cloned.1.call-update) | async-done | bytes 2359312 | tf_op jit(solution)/shard_map/all_gather | solution.py:29
  125.0 46.3 %all-gather.19.cloned.1.call-done = f32[32,96,192]{2,1,0:T(8,128)} async-done(((f32[2,96,192]{2,1,0:T(8,128)}), f32[32,96,192]{2,1,0:T(8,128)}) %all-gather.19.cloned.1.call-update) | async-done | bytes 2359312 | tf_op jit(solution)/shard_map/all_gather | solution.py:29
  171.3 46.2 %all-gather.13.cloned.1.call-done = f32[32,96,192]{2,1,0:T(8,128)} async-done(((f32[2,96,192]{2,1,0:T(8,128)}), f32[32,96,192]{2,1,0:T(8,128)}) %all-gather.13.cloned.1.call-update) | async-done | bytes 2359312 | tf_op jit(solution)/shard_map/all_gather | solution.py:29
  217.4 46.2 %all-gather.15.cloned.1.call-done = f32[32,96,192]{2,1,0:T(8,128)} async-done(((f32[2,96,192]{2,1,0:T(8,128)}), f32[32,96,192]{2,1,0:T(8,128)}) %all-gather.15.cloned.1.call-update) | async-done | bytes 2359312 | tf_op jit(solution)/shard_map/all_gather | solution.py:29
  263.6 24.2 %while.106 = (s32[]{:T(128)}, f32[2,96,192]{2,1,0:T(8,128)S(1)}, f32[2,96,192]{2,1,0:T(8,128)S(1)}, f32[2,96,192]{2,1,0:T(8,128)S(1)}, f32[2,96,192]{2,1,0:T(8,1...) while((s32[]{:T(128)}, f32[2,96,192]{2,1,0:T(8,128)S(1)}, ...), condition=%wide.region_9.10_spmd.clone, body=%wide.region_8.9_spmd.clone.sunk | while | flops 774148 | bytes 2211997 | solution.py:41
  265.1 1.5 fusion.31
  266.6 1.5 fusion.31
  268.2 1.5 fusion.31
  269.7 1.5 fusion.31
  274.2 1.5 fusion.31
  275.7 1.5 fusion.31
  277.3 1.5 fusion.31
  278.8 1.5 fusion.31
  280.3 1.5 fusion.31
  287.9 2.3 add_select_fusion
  290.2 93.3 %all-reduce.27.cloned.1.call-done = (f32[2,96,192]{2,1,0:T(8,128)}, f32[2,96,192]{2,1,0:T(8,128)}, f32[2,96,192]{2,1,0:T(8,128)}, f32[2,96,192]{2,1,0:T(8,128)}, f32[2,96,192]{2,1,0:T(8,128)}) async-done(((f32[2,96,192]{2,1,0:T(8,128)}, f32[2,96,192]{2,1,0:T(8,128)}, f32[2,96,192]{2,1,0:T(8,128)}, f32[2,96,192]{2,1,0:T(8,128)}, f32[2,96,192]{2,1,0:T(8,128)}), (f32[2,96,192]{2,1,0:T(8,128)}, ...) | async-done | bytes 737296 | tf_op jit(solution)/shard_map/psum | solution.py:46
  384.8 1.8 add_bitcast_fusion
  (177 shorter events, 34.5 us)
Async XLA Ops:
  6.5 2.5 copy-start.1
  6.5 72.1 %all-gather.11.cloned.1.call-start = ((), (), s32[]{:S(2)}) async-start(), calls=%async_computation | async-start | bytes 3342336 | tf_op jit(solution)/shard_map/all_gather | solution.py:29
  13.1 11.1 %collective-permute-start = (f32[2,2,96,192]{3,2,1,0:T(8,128)S(1)}, f32[2,2,96,192]{3,2,1,0:T(8,128)S(1)}, u32[]{:S(2)}, u32[]{:S(2)}) collective-permute-start(f32[2,2,96,192]{3,2,1,0:T(8,128)S(1)} %pad_maximum_fusion.1), channel_id=1, source_target_pairs={{0,1},{1,2},{2,3},{3,4},{4,5},{5,6},{6,7},{7,8},{8,9},{9,10},{10,1... | collective-permute-start | bytes 884744 | tf_op jit(solution)/shard_map/ppermute | solution.py:24
  21.5 10.6 %collective-permute-start.1 = (f32[2,2,96,192]{3,2,1,0:T(8,128)S(1)}, f32[2,2,96,192]{3,2,1,0:T(8,128)S(1)}, u32[]{:S(2)}, u32[]{:S(2)}) collective-permute-start(f32[2,2,96,192]{3,2,1,0:T(8,128)S(1)} %pad_maximum_fusion.2), channel_id=1, source_target_pairs={{0,1},{1,2},{2,3},{3,4},{4,5},{5,6},{6,7},{7,8},{8,9},{9,10},{10,1... | collective-permute-start | bytes 884744 | tf_op jit(solution)/shard_map/ppermute | solution.py:24
  33.2 3.7 copy-start
  34.3 90.7 %all-gather.17.cloned.1.call-start = ((), (), s32[]{:S(2)}) async-start(), calls=%async_computation.3 | async-start | bytes 3342336 | tf_op jit(solution)/shard_map/all_gather | solution.py:29
  35.0 136.2 %all-gather.19.cloned.1.call-start = ((), (), s32[]{:S(2)}) async-start(), calls=%async_computation.4 | async-start | bytes 3342336 | tf_op jit(solution)/shard_map/all_gather | solution.py:29
  35.8 181.7 %all-gather.13.cloned.1.call-start = ((), (), s32[]{:S(2)}) async-start(), calls=%async_computation.1 | async-start | bytes 3342336 | tf_op jit(solution)/shard_map/all_gather | solution.py:29
  36.3 227.3 %all-gather.15.cloned.1.call-start = ((), (), s32[]{:S(2)}) async-start(), calls=%async_computation.2 | async-start | bytes 3342336 | tf_op jit(solution)/shard_map/all_gather | solution.py:29
  36.9 346.6 %all-reduce.27.cloned.1.call-start = ((), (), s32[]{:S(2)}) async-start(), calls=%async_computation.5 | async-start | bytes 1966080 | tf_op jit(solution)/shard_map/psum | solution.py:46
Sparse Core Ops, SparseCore 0:
  34.4 44.1 all-gather.10
  80.9 43.9 all-gather.16
  127.2 43.9 all-gather.18
  173.4 43.9 all-gather.12
  219.6 43.9 all-gather.14
  290.3 93.1 all-reduce.26
where the time goes:
time: 395 us; the launch traced here: 394 us
  waiting for transfers between devices  326 us (83%)
  other arithmetic  47.5 us (12%)
  between operations  13.7 us (3%)
    all_gather x5, waiting for transfers between devices, prefix(): everything = jax.tree.map(lambda part: lax.all_gather(part, axis), value)  227 us
    psum x1, waiting for transfers between devices, broadcast(): return lax.psum(kept, axis)  93.3 us
    select_n x16, other arithmetic, lap(): return jax.tree.map(lambda a, b: jnp.where(reached, a, b), new, before)  23.9 us
    add x32, other arithmetic, fine_update(): recovery + time_step * recover_rate * (-recovery - excite_gain * potentia...  8.37 us
  transfers between devices with their start and end apart: 8, of which 7 were waited for; matrix products, arithmetic and copies ran while one was open for 3% of the time, Pallas kernels for 0%

commit v1 on v0

--- a/solution.py
+++ b/solution.py
@@ -22,28 +22,6 @@
     count = lax.axis_size(axis)
     pairs = [(source, (source + steps) % count) for source in range(count)]
     return lax.ppermute(value, axis, pairs)
-
-
-def prefix(value, axis, combine, identity):
-    size, here = (lax.axis_size(axis), lax.axis_index(axis))
-    everything = jax.tree.map(lambda part: lax.all_gather(part, axis), value)
-    start = jax.tree.map(
-        lambda part, zero: jnp.broadcast_to(jnp.asarray(zero, part.dtype), part.shape),
-        value,
-        identity,
-    )
-
-    def lap(k, before):
-        reached = k < here
-        new = combine(before, jax.tree.map(lambda part: part[k], everything))
-        return jax.tree.map(lambda a, b: jnp.where(reached, a, b), new, before)
-
-    return lax.fori_loop(0, size, lap, start)
-
-
-def broadcast(value, axis, source):
-    kept = jnp.where(lax.axis_index(axis) == source, value, 0).astype(value.dtype)
-    return lax.psum(kept, axis)
 
 
 def face_terms(labels):
@@ -151,6 +129,28 @@
     return (first_part, second)
 
 
+def solve_loop(own_map, size):
+    shape = own_map[0].shape
+    voxels = own_map[0].size
+    share = -(-voxels // size)
+    flat = jnp.stack(own_map).reshape(5, voxels)
+    flat = jnp.pad(flat, ((0, 0), (0, share * size - voxels)))
+    flat = flat.reshape(5, size, share).transpose(1, 0, 2)
+    maps = lax.all_to_all(flat, "tm", 0, 0)
+    maps = [[maps[k, f] for f in range(5)] for k in range(size)]
+    total = maps[0]
+    for mapping in maps[1:]:
+        total = compose(total, mapping)
+    state = loop_point(total)
+    entering = []
+    for mapping in maps:
+        entering.append(jnp.stack(state))
+        state = apply_map(mapping, state[0], state[1])
+    mine = lax.all_to_all(jnp.stack(entering), "tm", 0, 0)
+    mine = mine.transpose(1, 0, 2).reshape(2, size * share)[:, :voxels]
+    return mine.reshape((2,) + shape)
+
+
 def on_device(iterate, labels, stim_mask):
     loop_size = lax.axis_size("tm")
     slot_count = iterate.shape[0]
@@ -158,31 +158,27 @@
     beat_steps = loop_size * slot_count * MSTEPS
     face_coeffs = face_terms(labels)
     stimulus = pulse_height * stim_mask.astype(jnp.float32)
-    predicted = [
-        advance(iterate[offset], face_coeffs, stimulus, (first_slice + offset) * MSTEPS, beat_steps)
-        for offset in range(slot_count)
-    ]
-    incoming = from_behind(predicted[-1], "tm", 1)
+
+    def prop(state, offset):
+        return advance(state, face_coeffs, stimulus, (first_slice + offset) * MSTEPS, beat_steps)
+
+    predicted = [None] * slot_count
+    for offset in reversed(range(slot_count)):
+        predicted[offset] = prop(iterate[offset], offset)
+        if offset == slot_count - 1:
+            incoming = from_behind(predicted[offset], "tm", 1)
     relaxed = [incoming] + predicted[:-1]
-    propagated = [
-        advance(relaxed[offset], face_coeffs, stimulus, (first_slice + offset) * MSTEPS, beat_steps)
-        for offset in range(slot_count)
-    ]
-    arrived = from_behind(propagated[-1], "tm", 1)
+    propagated = [None] * slot_count
+    for offset in reversed(range(slot_count)):
+        propagated[offset] = prop(relaxed[offset], offset)
+        if offset == slot_count - 1:
+            arrived = from_behind(propagated[offset], "tm", 1)
     previous = [arrived] + propagated[:-1]
     slot_maps = [coarse_map(previous[offset], relaxed[offset]) for offset in range(slot_count)]
     own_map = slot_maps[0]
     for mapping in slot_maps[1:]:
         own_map = compose(own_map, mapping)
-    ones_field = jnp.ones(labels.shape, jnp.float32)
-    zero_field = jnp.zeros(labels.shape, jnp.float32)
-    identity = (ones_field, zero_field, ones_field, zero_field, zero_field)
-    before = prefix(own_map, "tm", compose, identity)
-    loop_map = jax.tree.map(
-        lambda part: broadcast(part, "tm", loop_size - 1), compose(before, own_map)
-    )
-    loop_state = loop_point(loop_map)
-    correction = apply_map(before, loop_state[0], loop_state[1])
+    correction = solve_loop(own_map, loop_size)
     results = []
     for offset in range(slot_count):
         correction = apply_map(slot_maps[offset], correction[0], correction[1])

time: 395 us -> 86.7 us (0.22)
  waiting for transfers between devices: 326 us -> 3.91 us
  blocking collectives: 0 us -> 46.8 us
  other arithmetic: 47.5 us -> 20.3 us
  between operations: 13.7 us -> 0.24 us
  local copies, waits for them, and re-layouts: 1.34 us -> 9.91 us
    all_gather x5 -> x0, waiting for transfers between devices: 227 us -> none  [prefix(): everything = jax.tree.map(lambda part: lax.all_gather(part, axis), value)]
    psum x1 -> x0, waiting for transfers between devices: 93.3 us -> none  [broadcast(): return lax.psum(kept, axis)]
    all_to_all x0 -> x2, blocking collectives: none -> 46.8 us  [the longest x1 33 us: solve_loop(): maps = lax.all_to_all(flat, 'tm', 0, 0)]
    select_n x17 -> x0, other arithmetic: 26.2 us -> none  [the longest x16 23.9 us: lap(): return jax.tree.map(lambda a, b: jnp.where(reached, a, b), new, before)]
    another operation x0 -> x6, local copies, waits for them, and re-layouts: none -> 7.45 us  [solve_loop(): flat = jnp.stack(own_map).reshape(5, voxels)]
  transfers between devices with their start and end apart: 8 -> 2, of which waited for: 7 -> 1; matrix products, arithmetic and copies ran while one was open for 3% -> 12% of each run, Pallas kernels for 0% -> 0%
where the time goes in v1:
time: 86.7 us; the launch traced here: 86.3 us
  blocking collectives  46.8 us (54%)
  other arithmetic  20.3 us (23%)
  local copies, waits for them, and re-layouts  9.91 us (11%)
  waiting for transfers between devices  3.91 us (5%)
  starting transfers between devices  3.19 us (4%)
  loops' own time  2 us (2%)
    all_to_all x1, blocking collectives, solve_loop(): maps = lax.all_to_all(flat, 'tm', 0, 0)  33 us
    all_to_all x1, blocking collectives, solve_loop(): mine = lax.all_to_all(jnp.stack(entering), 'tm', 0, 0)  13.8 us
    add x32, other arithmetic, fine_update(): recovery + time_step * recover_rate * (-recovery - excite_gain * potentia...  8.37 us
    another operation x6, local copies, waits for them, and re-layouts, solve_loop(): flat = jnp.stack(own_map).reshape(5, voxels)  7.45 us
    ppermute x2, waiting for transfers between devices, from_behind(): return lax.ppermute(value, axis, pairs)  3.91 us
    mul x32, other arithmetic, diffuse(): face_flux = along_z * (potential[:, :, 1:] - potential[:, :, :-1])  3.71 us
    ppermute x2, starting transfers between devices, from_behind(): return lax.ppermute(value, axis, pairs)  3.19 us
    another operation x4, loops' own time, advance(): lax.fori_loop(0, MSTEPS, one_step, (c_state[0], c_state[1]))  2 us
  transfers between devices with their start and end apart: 2, of which 1 were waited for; matrix products, arithmetic and copies ran while one was open for 12% of the time, Pallas kernels for 0%

profile of v1, /device:TPU:0, one launch (start us, length us, event | category | flops | bytes accessed | tf_op | source)
XLA Modules:
  0.0 86.3 jit_solution(3514046001077546793)
XLA Ops:
  0.0 1.1 %select_add_fusion = f32[2,96,192]{2,1,0:T(8,128)S(1)} fusion(s32[2,96,192]{2,1,0:T(8,128)} %param.12), kind=kLoop, calls=%fused_computation.97 | loop fusion | flops 405504 | bytes 294912 | tf_op jit(solution)/shard_map/add | solution.py:30
  1.4 3.9 %while.80 = (s32[]{:T(128)}, f32[2,96,192]{2,1,0:T(8,128)S(1)}, f32[2,96,192]{2,1,0:T(8,128)S(1)}, f32[1,96,192]{2,1,0:T(8,128)S(1)}, f32[2,95,192]{2,1,0:T(8,12...) while((s32[]{:T(128)}, f32[2,96,192]{2,1,0:T(8,128)S(1)}, ...), condition=%wide.region_1.2_spmd, body=%wide.region_0.1_spmd.sunk | while | flops 1289104 | bytes 2569256 | solution.py:86
  5.4 0.5 collective-permute-start
  5.9 3.9 %while.81 = (s32[]{:T(128)}, f32[2,96,192]{2,1,0:T(8,128)S(1)}, f32[2,96,192]{2,1,0:T(8,128)S(1)}, f32[1,96,192]{2,1,0:T(8,128)S(1)}, f32[2,95,192]{2,1,0:T(8,12...) while((s32[]{:T(128)}, f32[2,96,192]{2,1,0:T(8,128)S(1)}, ...), condition=%wide.region_3.4_spmd, body=%wide.region_2.3_spmd.sunk | while | flops 1289104 | bytes 2569256 | solution.py:86
  9.9 3.9 %while.82 = (s32[]{:T(128)}, f32[2,96,192]{2,1,0:T(8,128)S(1)}, f32[2,96,192]{2,1,0:T(8,128)S(1)}, f32[1,96,192]{2,1,0:T(8,128)S(1)}, f32[2,95,192]{2,1,0:T(8,12...) while((s32[]{:T(128)}, f32[2,96,192]{2,1,0:T(8,128)S(1)}, ...), condition=%wide.region_5.6_spmd, body=%wide.region_4.5_spmd.sunk | while | flops 1289104 | bytes 2569256 | solution.py:86
  13.8 2.7 %collective-permute-start.1 = (f32[2,2,96,192]{3,2,1,0:T(8,128)S(1)}, f32[2,2,96,192]{3,2,1,0:T(8,128)S(1)}, u32[]{:S(2)}, u32[]{:S(2)}) collective-permute-start(f32[2,2,96,192]{3,2,1,0:T(8,128)S(1)} %pad_maximum_fusion.2), channel_id=1, source_target_pairs={{0,1},{1,2},{2,3},{3,4},{4,5},{5,6},{6,7},{7,8},{8,9},{9,10},{10,1... | collective-permute-start | bytes 884744 | tf_op jit(solution)/shard_map/ppermute | solution.py:24
  16.6 3.9 %while.83 = (s32[]{:T(128)}, f32[2,96,192]{2,1,0:T(8,128)S(1)}, f32[2,96,192]{2,1,0:T(8,128)S(1)}, f32[1,96,192]{2,1,0:T(8,128)S(1)}, f32[2,95,192]{2,1,0:T(8,12...) while((s32[]{:T(128)}, f32[2,96,192]{2,1,0:T(8,128)S(1)}, ...), condition=%wide.region_7.8_spmd, body=%wide.region_6.7_spmd.sunk | while | flops 1289104 | bytes 2569256 | solution.py:86
  20.5 3.9 %collective-permute-done.1 = f32[2,2,96,192]{3,2,1,0:T(8,128)S(1)} collective-permute-done((f32[2,2,96,192]{3,2,1,0:T(8,128)S(1)}, f32[2,2,96,192]{3,2,1,0:T(8,128)S(1)}, u32[]{:S(2)}, u32[]{:S(2)}) %collective-permute-start.1) | collective-permute-done | bytes 294944 | tf_op jit(solution)/shard_map/ppermute | solution.py:24
  24.4 0.4 multiply_add_fusion.9
  24.8 0.8 stack.219
  25.6 0.8 stack.220
  26.9 0.4 copy-done
  27.3 0.8 stack.228
  28.1 0.8 stack.227
  29.0 0.9 stack.218
  29.8 3.2 %stack.229 = f32[5,16,2304]{2,0,1:T(8,128)S(1)} concatenate(f32[1,16,2304]{2,0,1:T(1,128)} %stack.218, f32[1,16,2304]{2,0,1:T(1,128)} %stack.219, f32[1,16,2304]{2,0,1:T(1,128)} %stack.220, f32[1,16,2304]{2,0,1:T(1,128)} %stack.227, f32[1,16,2304]{2,0,1:T(1,128)} %stack.228), dimensions={0} | concatenate | bytes 1474560 | tf_op jit(solution)/shard_map/stack | solution.py:136
  33.1 33.0 %all_to_all.10 = f32[16,5,2304]{2,1,0:T(8,128)S(1)} all-to-all(f32[16,5,2304]{2,1,0:T(8,128)S(1)} %bitcast.1006), channel_id=1, replica_groups=mesh['group'=2,'tm'=16] {'tm'}, dimensions={0} | all-to-all | bytes 1474560 | tf_op jit(solution)/shard_map/all_to_all | solution.py:139
  66.0 0.5 multiply_add_fusion.10
  66.5 1.0 %add_add_fusion.1 = (f32[1,2304]{1,0:T(1,128)S(1)}, f32[1,2304]{1,0:T(1,128)S(1)}, f32[1,2304]{1,0:T(1,128)S(1)}, f32[1,2304]{1,0:T(1,128)S(1)}, f32[1,2304]{1,0...) fusion(f32[1,2304]{1,0:T(1,128)S(1)} %get-tuple-element.1248, ...), kind=kLoop, calls=%fused_computation.222 | loop fusion | flops 493056 | bytes 1004544 | tf_op jit(solution)/shard_map/add | solution.py:122
  67.9 13.8 %all_to_all.11 = f32[16,2,2304]{2,1,0:T(2,128)S(1)} all-to-all(f32[16,2,2304]{2,1,0:T(2,128)S(1)} %constant_dynamic-update-slice_fusion), channel_id=1, replica_groups=mesh['group'=2,'tm'=16] {'tm'}, dimensions={0} | all-to-all | bytes 589824 | tf_op jit(solution)/shard_map/all_to_all | solution.py:149
  81.7 0.7 slice_reduce_fusion.1
  82.7 0.8 squeeze.377
  83.6 1.3 %add_bitcast_fusion = (f32[1,1,2,96,192]{4,3,2,1,0:T(8,128)S(1)}, f32[1,1,2,96,192]{4,3,2,1,0:T(8,128)S(1)}) fusion(f32[2,2,96,192]{3,2,1,0:T(8,128)S(1)} %copy-done.1, f32[2,2,96,192]{3,2,1,0:T(8,128)S(1)} %sub.842, f32[2,96,192]{2,1,0:T(8,128)S(1)} %get-tuple-element.1286, f32[2,96,192]{2,1,0:T(8,128)S(1)} %squeeze.376, ...), kind=kLoop, calls=%fused_computation.87 | loop fusion | flops 2101248 | bytes 1916928 | tf_op jit(solution)/shard_map/stack | solution.py:185
  85.3 1.0 %pad_maximum_fusion = f32[2,2,2,96,192]{4,3,2,1,0:T(8,128)} fusion(f32[1,2,2,96,192]{4,3,2,1,0:T(8,128)S(1)} %maximum_add_fusion.1, f32[1,2,2,96,192]{4,3,2,1,0:T(8,128)S(1)} %fusion), kind=kLoop, calls=%fused_computation.20 | loop fusion | flops 147456 | bytes 1179648 | tf_op jit(solution)/shard_map/stack | solution.py:186
  (171 shorter events, 15.6 us)
Async XLA Ops:
  0.0 1.3 %copy-start.3 = (s32[2,96,192]{2,1,0:T(8,128)S(1)}, s32[2,96,192]{2,1,0:T(8,128)}, u32[]{:S(2)}) copy-start(s32[2,96,192]{2,1,0:T(8,128)} %param.13) | copy-start | bytes 442372
  0.0 1.3 %copy-start.2 = (f32[2,2,2,96,192]{4,3,2,1,0:T(8,128)S(1)}, f32[2,2,2,96,192]{4,3,2,1,0:T(8,128)}, u32[]{:S(2)}) copy-start(f32[2,2,2,96,192]{4,3,2,1,0:T(8,128)} %param.11) | copy-start | bytes 1769476
  5.4 11.1 %collective-permute-start = (f32[2,2,96,192]{3,2,1,0:T(8,128)S(1)}, f32[2,2,96,192]{3,2,1,0:T(8,128)S(1)}, u32[]{:S(2)}, u32[]{:S(2)}) collective-permute-start(f32[2,2,96,192]{3,2,1,0:T(8,128)S(1)} %pad_maximum_fusion.1), channel_id=1, source_target_pairs={{0,1},{1,2},{2,3},{3,4},{4,5},{5,6},{6,7},{7,8},{8,9},{9,10},{10,1... | collective-permute-start | bytes 884744 | tf_op jit(solution)/shard_map/ppermute | solution.py:24
  13.8 10.6 %collective-permute-start.1 = (f32[2,2,96,192]{3,2,1,0:T(8,128)S(1)}, f32[2,2,96,192]{3,2,1,0:T(8,128)S(1)}, u32[]{:S(2)}, u32[]{:S(2)}) collective-permute-start(f32[2,2,96,192]{3,2,1,0:T(8,128)S(1)} %pad_maximum_fusion.2), channel_id=1, source_target_pairs={{0,1},{1,2},{2,3},{3,4},{4,5},{5,6},{6,7},{7,8},{8,9},{9,10},{10,1... | collective-permute-start | bytes 884744 | tf_op jit(solution)/shard_map/ppermute | solution.py:24
  26.5 0.7 copy-start
  67.9 15.7 %copy-start.1 = (f32[2,2,96,192]{3,2,1,0:T(8,128)S(1)}, f32[2,2,96,192]{3,2,1,0:T(8,128)}, u32[]{:S(2)}) copy-start(f32[2,2,96,192]{3,2,1,0:T(8,128)} %copy-done) | copy-start | bytes 884740

commit v2 on v1

v2 whole, which is shorter than its diff:
```python
import functools

import jax
import jax.numpy as jnp
from jax import lax
from jax.experimental import pallas as pl
from jax.experimental.pallas import tpu as pltpu
from jax.sharding import PartitionSpec as P

MSTEPS = 8
PULSE = 16
LANES = 128
ROWS = 8

time_step = 0.05
excite_gain = 8.0
threshold = 0.15
recovery_base = 0.005
recovery_gain = 0.2
recovery_shift = 0.3
pulse_height = 1.0
coarse_floor = -0.5
conduct_table = (0.1, 0.35, 0.7, 1.0)


def recovery_rate(potential, recovery):
    return recovery_base + recovery_gain * jnp.maximum(recovery, 0.0) / (
        jnp.maximum(potential, 0.0) + recovery_shift
    )


def compose(earlier, latter):
    return (
        latter[0] * earlier[0],
        latter[1] * earlier[0] + latter[2] * earlier[1],
        latter[2] * earlier[2],
        latter[0] * earlier[3] + latter[3],
        latter[1] * earlier[3] + latter[2] * earlier[4] + latter[4],
    )


def apply_map(mapping, first_in, second_in):
    return (
        mapping[0] * first_in + mapping[3],
        mapping[1] * first_in + mapping[2] * second_in + mapping[4],
    )


def loop_point(loop_map):
    first_part = loop_map[3] / (1.0 - loop_map[0])
    second = (loop_map[4] + loop_map[1] * first_part) / (1.0 - loop_map[2])
    return (first_part, second)


def neighbours(ref, slot, tile, lane):
    here = pl.ds(ROWS + ROWS * tile, ROWS)
    above = pl.ds(ROWS - 1 + ROWS * tile, ROWS)
    below = pl.ds(ROWS + 1 + ROWS * tile, ROWS)
    mid = [ref[slot, k, here] for k in range(3)]
    up = [ref[slot, k, above] for k in range(3)]
    down = [ref[slot, k, below] for k in range(3)]
    first, second, rest = mid
    swapped = pltpu.roll(rest, 64, 1)
    first_left = pltpu.roll(first, 1, 1)
    rest_right = pltpu.roll(rest, LANES - 1, 1)
    left = [
        first_left,
        pltpu.roll(second, 1, 1),
        jnp.where(
            lane == 0,
            first_left,
            jnp.where(lane == 64, pltpu.roll(second, 65, 1), pltpu.roll(rest, 1, 1)),
        ),
    ]
    right = [
        jnp.where(lane == LANES - 1, rest_right, pltpu.roll(first, LANES - 1, 1)),
        jnp.where(
            lane == LANES - 1,
            pltpu.roll(swapped, LANES - 1, 1),
            pltpu.roll(second, LANES - 1, 1),
        ),
        rest_right,
    ]
    return mid, up, down, left, right, [second, first, swapped]


def slot_map(prev_p, prev_q, relax_p, relax_q):
    potential = jnp.clip(prev_p, 0.0, 1.0)
    recovery = jnp.maximum(prev_q, 0.0)
    recover_rate = recovery_rate(potential, recovery)
    horizon = MSTEPS * time_step
    fast_slope = jnp.minimum(
        -excite_gain
        * (3.0 * potential * potential - 2.0 * (1.0 + threshold) * potential + threshold)
        - recovery,
        coarse_floor,
    )
    cross_term = -recover_rate * excite_gain * (2.0 * potential - threshold - 1.0)
    first_diag = 1.0 / (1.0 - horizon * fast_slope)
    second_diag = 1.0 / (1.0 + horizon * recover_rate)
    lower_term = horizon * cross_term * first_diag * second_diag
    return (first_diag, lower_term, second_diag, prev_p - relax_p, prev_q - relax_q)


def kernel(
    loop_size, chips, groups,
    it_ref, conduct_ref, stim_ref, out_ref,
    pot, rec, cond, coef, relaxed, previous, sent, maps, own, got, early, pair,
    parts, total, totals, leave, enter, pass_on, entry,
    ring_s, ring_r, a_s, a_r, b_s, b_r, g_s, g_r, c_s, c_r, d_s, d_r,
):
    slots = it_ref.shape[0]
    tiles = conduct_ref.shape[1] // ROWS
    half = tiles // 2
    me = lax.axis_index("tm")
    core = lax.rem(me, 2)
    chip = lax.rem(me // 2, chips)
    group = me // (2 * chips)
    base = group * 2 * chips
    partner = me + 1 - 2 * core
    right = lax.rem(me + 1, loop_size)
    across = lax.rem(me + 2 * core - 1 + loop_size, loop_size)
    owner = jnp.logical_and(chip != 1, chip != chips - 2)
    my_tile = chip - (chip + chips - 1) // chips - (chip + 2) // chips

    barrier = pltpu.get_barrier_semaphore()

    def greet(device):
        pl.semaphore_signal(
            barrier, inc=1, device_id={"tm": device}, device_id_type=pl.DeviceIdType.MESH
        )

    greet(partner)
    greet(across)
    for hop in range(1, chips):
        greet(base + 2 * lax.rem(chip + hop, chips) + core)
    for hop in range(1, groups):
        greet(lax.rem(me + hop * 2 * chips, loop_size))

    def remote(source, target, send_sem, recv_sem, device):
        return pltpu.make_async_remote_copy(
            src_ref=source, dst_ref=target, send_sem=send_sem, recv_sem=recv_sem,
            device_id={"tm": device}, device_id_type=pl.DeviceIdType.MESH,
        )

    lane = lax.broadcasted_iota(jnp.int32, (ROWS, LANES), 1)
    row = lax.broadcasted_iota(jnp.int32, (ROWS, LANES), 0)
    edge = jnp.zeros((ROWS, LANES), jnp.float32)
    for k in range(3):
        for end in (0, ROWS + ROWS * tiles):
            cond[0, k, pl.ds(end, ROWS)] = edge
            pot[0, k, pl.ds(end, ROWS)] = edge
            pot[1, k, pl.ds(end, ROWS)] = edge
        cond[0, k, pl.ds(ROWS, ROWS * tiles)] = conduct_ref[k]
    for t in range(tiles):
        mid, up, down, left, right_, over = neighbours(cond, 0, t, lane)
        here = pl.ds(ROWS * t, ROWS)
        for k in range(3):
            def face(value, open_face=None):
                mean = time_step * 0.5 * (mid[k] + value)
                return mean if open_face is None else jnp.where(open_face, mean, 0.0)

            faces = (
                face(up[k], row > 0 if t == 0 else None),
                face(down[k], row < ROWS - 1 if t == tiles - 1 else None),
                face(left[k], lane > 0 if k < 2 else None),
                face(
                    right_[k],
                    None if k < 2 else jnp.logical_and(lane != 63, lane != LANES - 1),
                ),
                face(over[k]),
            )
            for n, value in enumerate(faces):
                coef[n, k, here] = value
            coef[5, k, here] = 1.0 - (((faces[0] + faces[1]) + (faces[2] + faces[3])) + faces[4])

    def advance(source, target, slice_index):
        for k in range(3):
            pot[0, k, pl.ds(ROWS, ROWS * tiles)] = source[0, k]
            rec[k] = source[1, k]

        def one_step(step, carry):
            moment = lax.rem(slice_index * MSTEPS + step, loop_size * slots * MSTEPS)
            switch = jnp.where(moment < PULSE, time_step * pulse_height, 0.0)
            now = lax.rem(step, 2)
            for t in range(tiles):
                mid, up, down, left, right_, over = neighbours(pot, now, t, lane)
                here = pl.ds(ROWS * t, ROWS)
                for k in range(3):
                    p, q = mid[k], rec[k, here]
                    flow = coef[0, k, here] * up[k] + coef[1, k, here] * down[k]
                    flow = flow + (coef[2, k, here] * left[k] + coef[3, k, here] * right_[k])
                    flow = flow + (coef[4, k, here] * over[k] + switch * stim_ref[k, here])
                    gain = (p - threshold) * (p - 1.0)
                    keep = coef[5, k, here] - time_step * (excite_gain * gain + q)
                    pot[1 - now, k, pl.ds(ROWS + ROWS * t, ROWS)] = p * keep + flow
                    rate = time_step * recovery_rate(p, q)
                    pull = q + excite_gain * p * (p - (threshold + 1.0))
                    rec[k, here] = q - rate * pull
            return carry

        lax.fori_loop(0, MSTEPS, one_step, 0)
        for k in range(3):
            target[0, k] = pot[MSTEPS % 2, k, pl.ds(ROWS, ROWS * tiles)]
            target[1, k] = rec[k]

    first_slice = me * slots
    last = slots - 1
    advance(it_ref.at[last], sent.at[0], first_slice + last)
    pl.semaphore_wait(barrier, chips + 1 + groups - 1)
    ring_one = remote(sent.at[0], relaxed.at[0], ring_s.at[0], ring_r.at[0], right)
    ring_one.start()
    for s in reversed(range(last)):
        advance(it_ref.at[s], relaxed.at[s + 1], first_slice + s)
    ring_two = remote(sent.at[1], previous.at[0], ring_s.at[1], ring_r.at[1], right)
    for s in reversed(range(slots)):
        if s == 0:
            ring_one.wait_recv()
        if s == last:
            advance(relaxed.at[s], sent.at[1], first_slice + s)
            ring_two.start()
        else:
            advance(relaxed.at[s], previous.at[s + 1], first_slice + s)
    ring_two.wait_recv()

    def make_maps(t):
        here = pl.ds(pl.multiple_of(ROWS * t, ROWS), ROWS)
        for k in range(3):
            whole = None
            for s in range(slots):
                mapping = slot_map(
                    previous[s, 0, k, here], previous[s, 1, k, here],
                    relaxed[s, 0, k, here], relaxed[s, 1, k, here],
                )
                for n in range(5):
                    maps[s, t, n, k] = mapping[n]
                whole = mapping if whole is None else compose(whole, mapping)
            for n in range(5):
                own[t, n, k] = whole[n]

    def fields(ref, *place):
        return tuple(ref[(*place, n)] for n in range(5))

    def a_copy(j):
        return remote(
            own.at[half * (1 - core) + j], got.at[j], a_s.at[j], a_r.at[j], partner
        )

    def phase_send(j, carry):
        make_maps(half * (1 - core) + j)
        a_copy(j).start()
        return carry

    def phase_keep(j, carry):
        make_maps(half * core + j)
        return carry

    lax.fori_loop(0, half, phase_send, 0)
    lax.fori_loop(0, half, phase_keep, 0)

    def owner_of(j):
        return j + (j + half - 1) // half + (j + 1) // half

    def b_copy(j):
        return remote(
            pair.at[j], parts.at[chip], b_s.at[j], b_r.at[chip],
            base + 2 * owner_of(j) + core,
        )

    def phase_pair(turn, carry):
        j = lax.rem(turn + chip, half)
        a_copy(j).wait_recv()
        for k in range(3):
            mine = tuple(own[half * core + j, n, k] for n in range(5))
            theirs = tuple(got[j, n, k] for n in range(5))
            is_first = core == 0
            earlier = tuple(jnp.where(is_first, m, h) for m, h in zip(mine, theirs))
            later = tuple(jnp.where(is_first, h, m) for m, h in zip(mine, theirs))
            both = compose(earlier, later)
            for n in range(5):
                early[j, n, k] = earlier[n]
                pair[j, n, k] = both[n]

        @pl.when(owner_of(j) != chip)
        def _():
            b_copy(j).start()

        @pl.when(owner_of(j) == chip)
        def _():
            parts[chip] = pair[j]

        return carry

    lax.fori_loop(0, half, phase_pair, 0)

    def c_copy(k):
        return remote(
            leave.at[k], enter.at[my_tile], c_s.at[k], c_r.at[my_tile], base + 2 * k + core
        )

    @pl.when(owner)
    def _():
        for k in range(chips):
            @pl.when(chip != k)
            def _():
                remote(
                    pair.at[0], parts.at[k], b_s.at[0], b_r.at[k], base + 2 * k + core
                ).wait_recv()

        whole = fields(parts, 0)
        for k in range(1, chips):
            whole = compose(whole, fields(parts, k))
        if groups == 1:
            state = loop_point(whole)
        else:
            total[...] = jnp.stack(whole)
            totals[group] = total[...]

            def g_copy(hop):
                to = lax.rem(me + hop * 2 * chips, loop_size)
                return remote(total, totals.at[group], g_s.at[hop], g_r.at[hop], to)

            for hop in range(1, groups):
                g_copy(hop).start()
            for hop in range(1, groups):
                g_copy(hop).wait()
            whole = fields(totals, 0)
            for g in range(1, groups):
                whole = compose(whole, fields(totals, g))
            state = loop_point(whole)
            for g in range(groups - 1):
                after = apply_map(fields(totals, g), state[0], state[1])
                state = tuple(jnp.where(g < group, n, o) for n, o in zip(after, state))
        for k in range(chips):
            leave[k, 0] = state[0]
            leave[k, 1] = state[1]

            @pl.when(chip != k)
            def _():
                c_copy(k).start()

            @pl.when(chip == k)
            def _():
                enter[my_tile] = leave[k]

            if k < chips - 1:
                state = apply_map(fields(parts, k), state[0], state[1])

    def finish(t):
        here = pl.ds(pl.multiple_of(ROWS * t, ROWS), ROWS)
        for k in range(3):
            value = (entry[t, 0, k], entry[t, 1, k])
            for s in range(slots):
                mapping = tuple(maps[s, t, n, k] for n in range(5))
                value = apply_map(mapping, value[0], value[1])
                out_ref[s, 0, k, here] = relaxed[s, 0, k, here] + value[0]
                out_ref[s, 1, k, here] = relaxed[s, 1, k, here] + value[1]

    def d_copy(j):
        return remote(pass_on.at[j], entry.at[half * core + j], d_s.at[j], d_r.at[j], partner)

    def phase_back(j, carry):
        @pl.when(owner_of(j) != chip)
        def _():
            remote(
                leave.at[0], enter.at[j], c_s.at[0], c_r.at[j], base + 2 * owner_of(j) + core
            ).wait_recv()

        for k in range(3):
            zero = (enter[j, 0, k], enter[j, 1, k])
            one = apply_map(tuple(early[j, n, k] for n in range(5)), zero[0], zero[1])
            for n in range(2):
                entry[half * core + j, n, k] = jnp.where(core == 0, zero[n], one[n])
                pass_on[j, n, k] = jnp.where(core == 0, one[n], zero[n])
        d_copy(j).start()
        return carry

    lax.fori_loop(0, half, phase_back, 0)

    def phase_mine(j, carry):
        finish(half * core + j)
        return carry

    def phase_theirs(j, carry):
        remote(
            pass_on.at[j], entry.at[half * (1 - core) + j], d_s.at[j], d_r.at[j], partner
        ).wait_recv()
        finish(half * (1 - core) + j)
        return carry

    lax.fori_loop(0, half, phase_mine, 0)
    lax.fori_loop(0, half, phase_theirs, 0)

    ring_one.wait_send()
    ring_two.wait_send()
    for j in range(half):
        a_copy(j).wait_send()
        d_copy(j).wait_send()

        @pl.when(owner_of(j) != chip)
        def _():
            b_copy(j).wait_send()

    @pl.when(owner)
    def _():
        for k in range(chips):
            @pl.when(chip != k)
            def _():
                c_copy(k).wait_send()


def pack(field):
    rest = field[..., LANES:]
    rest = jnp.concatenate([rest[..., 0, :, :], rest[..., 1, :, :]], axis=-1)
    return jnp.concatenate([field[..., :LANES], rest[..., None, :, :]], axis=-3)


def unpack(packed):
    rest = packed[..., 2, :, :]
    rest = jnp.stack([rest[..., : LANES // 2], rest[..., LANES // 2 :]], axis=-3)
    return jnp.concatenate([packed[..., :2, :, :], rest], axis=-1)


def on_device(iterate, labels, stim_mask):
    loop_size = lax.axis_size("tm")
    chips = 8
    groups = loop_size // (2 * chips)
    slots = iterate.shape[0]
    conduct = jnp.zeros(labels.shape, jnp.float32)
    for label_id, conduct_value in enumerate(conduct_table):
        conduct = jnp.where(labels == label_id, jnp.float32(conduct_value), conduct)
    state = pack(iterate)
    rows = labels.shape[1]
    tiles = rows // ROWS
    half = tiles // 2
    f32 = jnp.float32
    block = (3, ROWS, LANES)
    dma = pltpu.SemaphoreType.DMA
    out = pl.pallas_call(
        functools.partial(kernel, loop_size, chips, groups),
        out_shape=jax.ShapeDtypeStruct(state.shape, f32),
        in_specs=[pl.BlockSpec(memory_space=pltpu.VMEM)] * 3,
        out_specs=pl.BlockSpec(memory_space=pltpu.VMEM),
        scratch_shapes=[
            pltpu.VMEM((2, 3, rows + 2 * ROWS, LANES), f32),
            pltpu.VMEM((3, rows, LANES), f32),
            pltpu.VMEM((1, 3, rows + 2 * ROWS, LANES), f32),
            pltpu.VMEM((6, 3, rows, LANES), f32),
            pltpu.VMEM(state.shape, f32),
            pltpu.VMEM(state.shape, f32),
            pltpu.VMEM((2, 2, 3, rows, LANES), f32),
            pltpu.VMEM((slots, tiles, 5) + block, f32),
            pltpu.VMEM((tiles, 5) + block, f32),
            pltpu.VMEM((half, 5) + block, f32),
            pltpu.VMEM((half, 5) + block, f32),
            pltpu.VMEM((half, 5) + block, f32),
            pltpu.VMEM((chips, 5) + block, f32),
            pltpu.VMEM((5,) + block, f32),
            pltpu.VMEM((groups, 5) + block, f32),
            pltpu.VMEM((chips, 2) + block, f32),
            pltpu.VMEM((half, 2) + block, f32),
            pltpu.VMEM((half, 2) + block, f32),
            pltpu.VMEM((tiles, 2) + block, f32),
            dma((2,)), dma((2,)),
            dma((half,)), dma((half,)),
            dma((half,)), dma((chips,)),
            dma((groups,)), dma((groups,)),
            dma((chips,)), dma((half,)),
            dma((half,)), dma((half,)),
        ],
        compiler_params=pltpu.CompilerParams(
            collective_id=0, has_side_effects=True, vmem_limit_bytes=32 * 1024 * 1024
        ),
    )(state, pack(conduct), pack(stim_mask.astype(f32)))
    return unpack(out)


def solution(mesh):
    in_specs = (
        P(("group", "tm"), None, None, None, None),
        P("group", None, None),
        P("group", None, None),
    )
    out_specs = P(("group", "tm"), None, None, None, None)
    return jax.shard_map(
        on_device, mesh=mesh, in_specs=in_specs, out_specs=out_specs, check_vma=False
    )
```

time: 86.7 us -> 41.9 us (0.48)
  blocking collectives: 46.8 us -> 0 us
  Pallas kernels: 0 us -> 35.6 us
  other arithmetic: 20.3 us -> 2.28 us
  local copies, waits for them, and re-layouts: 9.91 us -> 3.64 us
  waiting for transfers between devices: 3.91 us -> 0 us
  starting transfers between devices: 3.19 us -> 0 us
  loops' own time: 2 us -> 0 us
    all_to_all x2 -> x0, blocking collectives: 46.8 us -> none  [the longest x1 33 us: solve_loop(): maps = lax.all_to_all(flat, 'tm', 0, 0)]
    pallas_call x0 -> x1, Pallas kernels: none -> 35.6 us  [on_device(): pl.pallas_call(functools.partial(kernel, loop_size, chips, groups), out_s...]
    add x39 -> x0, other arithmetic: 11.8 us -> none  [the longest x32 8.37 us: fine_update(): recovery + time_step * recover_rate * (-recovery - excite_gain * potentia...]
    another operation x6 -> x1, local copies, waits for them, and re-layouts: 7.45 us -> 0.11 us  [unpack(): rest = jnp.stack([rest[..., :LANES // 2], rest[..., LANES // 2:]], axis=-3)]
    mul x99 -> x0, other arithmetic: 5.51 us -> none  [the longest x32 3.71 us: diffuse(): face_flux = along_z * (potential[:, :, 1:] - potential[:, :, :-1])]
    ppermute x2 -> x0, waiting for transfers between devices: 3.91 us -> none  [from_behind(): return lax.ppermute(value, axis, pairs)]
    ppermute x2 -> x0, starting transfers between devices: 3.19 us -> none  [from_behind(): return lax.ppermute(value, axis, pairs)]
    another operation x6 -> x0, other arithmetic: 2.41 us -> none  [the longest x1 1.31 us: on_device(): results.append(relaxed[offset] + jnp.stack(correction))]
  transfers between devices with their start and end apart: 2 -> 0, of which waited for: 1 -> 0; matrix products, arithmetic and copies ran while one was open for 12% -> 0% of each run, Pallas kernels for 0% -> 0%
where the time goes in v2:
time: 41.9 us; the launch traced here: 41.7 us
  Pallas kernels  35.6 us (85%)
  local copies, waits for them, and re-layouts  3.64 us (9%)
  other arithmetic  2.28 us (5%)
    pallas_call x1, Pallas kernels, on_device(): pl.pallas_call(functools.partial(kernel, loop_size, chips, groups), out_s...  35.6 us
    unnamed x6, local copies, waits for them, and re-layouts  1.79 us
    slice x5, local copies, waits for them, and re-layouts, pack(): return jnp.concatenate([field[..., :LANES], rest[..., None, :, :]], axis=-3)  1.65 us
    select_n x1, other arithmetic, on_device(): conduct = jnp.where(labels == label_id, jnp.float32(conduct_value), conduct)  0.98 us
    concatenate x1, other arithmetic, unpack(): return jnp.concatenate([packed[..., :2, :, :], rest], axis=-1)  0.94 us

profile of v2, /device:TPU:0, one launch (start us, length us, event | category | flops | bytes accessed | tf_op | source)
XLA Modules:
  0.0 41.7 jit_solution(16203697644770109637)
XLA Ops:
  0.0 1.0 %select_select_fusion = f32[2,96,192]{2,1,0:T(8,128)S(1)} fusion(s32[2,96,192]{2,1,0:T(8,128)} %param.4), kind=kLoop, calls=%fused_computation.7 | loop fusion | flops 294912 | bytes 294912 | tf_op jit(solution)/shard_map/jit(_where)/select_n | solution.py:431
  1.0 0.0 copy-start.1
  1.0 0.7 %copy-done.1 = f32[2,96,192]{2,1,0:T(8,128)} copy-done((f32[2,96,192]{2,1,0:T(8,128)}, f32[2,96,192]{2,1,0:T(8,128)S(1)}, u32[]{:S(2)}) %copy-start.1) | copy-done | bytes 147480
  1.7 0.0 copy-start.2
  1.7 0.1 maximum_bitcast_fusion.1
  1.8 0.8 %copy-done.2 = s32[2,96,192]{2,1,0:T(8,128)S(1)} copy-done((s32[2,96,192]{2,1,0:T(8,128)S(1)}, s32[2,96,192]{2,1,0:T(8,128)}, u32[]{:S(2)}) %copy-start.2) | copy-done | bytes 147480
  2.6 0.0 slice-start.1
  2.7 0.0 copy-start
  2.7 0.1 maximum_bitcast_fusion.2
  2.7 0.8 %slice-done.1 = f32[2,96,128]{2,1,0:T(8,128)S(1)} async-done(((f32[2,96,192]{2,1,0:T(8,128)}), f32[2,96,128]{2,1,0:T(8,128)S(1)}, s32[]{:S(2)}) %slice-start.1) | async-done | bytes 98328 | tf_op jit(solution)/shard_map/slice | solution.py:415
  3.5 0.3 copy-done
  3.9 0.0 slice-start
  3.9 0.1 maximum_bitcast_fusion
  4.0 0.9 %slice-done = f32[2,2,2,96,128]{4,3,2,1,0:T(8,128)S(1)} async-done(((f32[2,2,2,96,192]{4,3,2,1,0:T(8,128)}), f32[2,2,2,96,128]{4,3,2,1,0:T(8,128)S(1)}, s32[]{:S(2)}) %slice-start) | async-done | bytes 393240 | tf_op jit(solution)/shard_map/slice | solution.py:415
  4.9 35.6 %shard_map.37 = f32[2,2,3,96,128]{4,3,2,1,0:T(8,128)S(1)} custom-call(f32[2,2,3,96,128]{4,3,2,1,0:T(8,128)S(1)} %pad_maximum_fusion.1.it_ref, f32[3,96,128]{2,1,0:T(8,128)S(1)} %get-tuple-element.13.conduct_ref, f32[3,96,128]{2,1,0:T(8,128)S(1)} %get-tuple-element.14.stim_ref), custom_call_target="tpu_custom_call" | custom-call | tf_op jit(solution)/shard_map/pallas_call | solution.py:439
  40.6 0.1 slice_bitcast_fusion.1
  40.7 0.9 %pad_maximum_fusion = f32[2,2,2,96,192]{4,3,2,1,0:T(8,128)} fusion(f32[2,2,2,96,128]{4,3,2,1,0:T(8,128)S(1)} %slice.57, f32[2,2,1,96,64]{4,3,1,0,2:T(8,128)S(1)} %get-tuple-element.8, f32[2,2,1,96,64]{4,3,1,0,2:T(8,128)S(1)} %get-tuple-element.7), kind=kLoop, calls=%fused_computation | loop fusion | flops 196608 | bytes 1179648 | tf_op jit(solution)/shard_map/concatenate | solution.py:421
  (9 shorter events, 0.2 us)
Async XLA Ops:
  1.0 0.7 %copy-start.1 = (f32[2,96,192]{2,1,0:T(8,128)}, f32[2,96,192]{2,1,0:T(8,128)S(1)}, u32[]{:S(2)}) copy-start(f32[2,96,192]{2,1,0:T(8,128)S(1)} %select_select_fusion) | copy-start | bytes 442372
  1.7 0.9 %copy-start.2 = (s32[2,96,192]{2,1,0:T(8,128)S(1)}, s32[2,96,192]{2,1,0:T(8,128)}, u32[]{:S(2)}) copy-start(s32[2,96,192]{2,1,0:T(8,128)} %param.5) | copy-start | bytes 442372
  2.6 0.9 %slice-start.1 = ((f32[2,96,192]{2,1,0:T(8,128)}), f32[2,96,128]{2,1,0:T(8,128)S(1)}, s32[]{:S(2)}) async-start(f32[2,96,192]{2,1,0:T(8,128)} %copy-done.1), calls=%async_computation.1 | async-start | bytes 196608 | tf_op jit(solution)/shard_map/slice | solution.py:415
  2.7 1.2 %copy-start = (f32[2,2,2,96,192]{4,3,2,1,0:T(8,128)S(1)}, f32[2,2,2,96,192]{4,3,2,1,0:T(8,128)}, u32[]{:S(2)}) copy-start(f32[2,2,2,96,192]{4,3,2,1,0:T(8,128)} %param.3) | copy-start | bytes 1769476
  3.9 1.0 %slice-start = ((f32[2,2,2,96,192]{4,3,2,1,0:T(8,128)}), f32[2,2,2,96,128]{4,3,2,1,0:T(8,128)S(1)}, s32[]{:S(2)}) async-start(f32[2,2,2,96,192]{4,3,2,1,0:T(8,128)} %param.3), calls=%async_computation | async-start | bytes 786432 | tf_op jit(solution)/shard_map/slice | solution.py:415

commit v3 on v2

--- a/solution.py
+++ b/solution.py
@@ -23,10 +23,14 @@
 conduct_table = (0.1, 0.35, 0.7, 1.0)
 
 
-def recovery_rate(potential, recovery):
-    return recovery_base + recovery_gain * jnp.maximum(recovery, 0.0) / (
-        jnp.maximum(potential, 0.0) + recovery_shift
-    )
+def inverse(value):
+    guess = pl.reciprocal(value, approx=True)
+    return guess * (2.0 - value * guess)
+
+
+def scaled_rate(potential, recovery, scale):
+    above = (scale * recovery_gain) * jnp.maximum(recovery, 0.0)
+    return scale * recovery_base + above * inverse(jnp.maximum(potential, 0.0) + recovery_shift)
 
 
 def compose(earlier, latter):
@@ -84,10 +88,16 @@
     return mid, up, down, left, right, [second, first, swapped]
 
 
+def packed(ref, place, here):
+    first, second = ref[(*place, 0, here)], ref[(*place, 1, here)]
+    rest = jnp.concatenate([first[:, LANES:], second[:, LANES:]], axis=1)
+    return [first[:, :LANES], second[:, :LANES], rest]
+
+
 def slot_map(prev_p, prev_q, relax_p, relax_q):
     potential = jnp.clip(prev_p, 0.0, 1.0)
     recovery = jnp.maximum(prev_q, 0.0)
-    recover_rate = recovery_rate(potential, recovery)
+    recover_rate = scaled_rate(potential, recovery, 1.0)
     horizon = MSTEPS * time_step
     fast_slope = jnp.minimum(
         -excite_gain
@@ -96,21 +106,31 @@
         coarse_floor,
     )
     cross_term = -recover_rate * excite_gain * (2.0 * potential - threshold - 1.0)
-    first_diag = 1.0 / (1.0 - horizon * fast_slope)
-    second_diag = 1.0 / (1.0 + horizon * recover_rate)
+    first_diag = inverse(1.0 - horizon * fast_slope)
+    second_diag = inverse(1.0 + horizon * recover_rate)
     lower_term = horizon * cross_term * first_diag * second_diag
     return (first_diag, lower_term, second_diag, prev_p - relax_p, prev_q - relax_q)
 
 
 def kernel(
     loop_size, chips, groups,
-    it_ref, conduct_ref, stim_ref, out_ref,
-    pot, rec, cond, coef, relaxed, previous, sent, maps, own, got, early, pair,
+    iterate_hbm, labels_hbm, stim_hbm, out_ref,
+    raw, raw_labels, raw_stim, it_ref, stim_ref, load_sem,
+    pot, rec, drive, cond, coef, relaxed, previous, sent, maps, own, got, early, pair,
     parts, total, totals, leave, enter, pass_on, entry,
     ring_s, ring_r, a_s, a_r, b_s, b_r, g_s, g_r, c_s, c_r, d_s, d_r,
 ):
     slots = it_ref.shape[0]
-    tiles = conduct_ref.shape[1] // ROWS
+    tiles = stim_ref.shape[1] // ROWS
+    last = slots - 1
+    loads = [
+        pltpu.make_async_copy(labels_hbm, raw_labels, load_sem.at[slots]),
+        pltpu.make_async_copy(stim_hbm, raw_stim, load_sem.at[slots + 1]),
+    ]
+    for s in reversed(range(slots)):
+        loads.append(pltpu.make_async_copy(iterate_hbm.at[s], raw.at[s], load_sem.at[s]))
+    for load in loads:
+        load.start()
     half = tiles // 2
     me = lax.axis_index("tm")
     core = lax.rem(me, 2)
@@ -151,7 +171,19 @@
             cond[0, k, pl.ds(end, ROWS)] = edge
             pot[0, k, pl.ds(end, ROWS)] = edge
             pot[1, k, pl.ds(end, ROWS)] = edge
-        cond[0, k, pl.ds(ROWS, ROWS * tiles)] = conduct_ref[k]
+    loads[0].wait()
+    for t in range(tiles):
+        here = pl.ds(ROWS * t, ROWS)
+        for k, label in enumerate(packed(raw_labels, (), here)):
+            conduct = jnp.full((ROWS, LANES), conduct_table[0], jnp.float32)
+            for label_id in range(1, len(conduct_table)):
+                conduct = jnp.where(label == label_id, conduct_table[label_id], conduct)
+            cond[0, k, pl.ds(ROWS + ROWS * t, ROWS)] = conduct
+    loads[1].wait()
+    for t in range(tiles):
+        here = pl.ds(ROWS * t, ROWS)
+        for k, mask in enumerate(packed(raw_stim, (), here)):
+            stim_ref[k, here] = mask.astype(jnp.float32)
     for t in range(tiles):
         mid, up, down, left, right_, over = neighbours(cond, 0, t, lane)
         here = pl.ds(ROWS * t, ROWS)
@@ -172,16 +204,25 @@
             )
             for n, value in enumerate(faces):
                 coef[n, k, here] = value
-            coef[5, k, here] = 1.0 - (((faces[0] + faces[1]) + (faces[2] + faces[3])) + faces[4])
+            stay = 1.0 - time_step * excite_gain * threshold
+            coef[5, k, here] = stay - (((faces[0] + faces[1]) + (faces[2] + faces[3])) + faces[4])
+
+    def unload(s):
+        loads[2 + last - s].wait()
+        for n in range(2):
+            for t in range(tiles):
+                here = pl.ds(ROWS * t, ROWS)
+                for k, value in enumerate(packed(raw, (s, n), here)):
+                    it_ref[s, n, k, here] = value
 
     def advance(source, target, slice_index):
+        switch = jnp.where(slice_index * MSTEPS < PULSE, time_step * pulse_height, 0.0)
         for k in range(3):
             pot[0, k, pl.ds(ROWS, ROWS * tiles)] = source[0, k]
             rec[k] = source[1, k]
+            drive[k] = switch * stim_ref[k]
 
         def one_step(step, carry):
-            moment = lax.rem(slice_index * MSTEPS + step, loop_size * slots * MSTEPS)
-            switch = jnp.where(moment < PULSE, time_step * pulse_height, 0.0)
             now = lax.rem(step, 2)
             for t in range(tiles):
                 mid, up, down, left, right_, over = neighbours(pot, now, t, lane)
@@ -190,13 +231,11 @@
                     p, q = mid[k], rec[k, here]
                     flow = coef[0, k, here] * up[k] + coef[1, k, here] * down[k]
                     flow = flow + (coef[2, k, here] * left[k] + coef[3, k, here] * right_[k])
-                    flow = flow + (coef[4, k, here] * over[k] + switch * stim_ref[k, here])
-                    gain = (p - threshold) * (p - 1.0)
-                    keep = coef[5, k, here] - time_step * (excite_gain * gain + q)
+                    flow = flow + (coef[4, k, here] * over[k] + drive[k, here])
+                    pull = q + excite_gain * (p * (p - (threshold + 1.0)))
+                    keep = coef[5, k, here] - time_step * pull
                     pot[1 - now, k, pl.ds(ROWS + ROWS * t, ROWS)] = p * keep + flow
-                    rate = time_step * recovery_rate(p, q)
-                    pull = q + excite_gain * p * (p - (threshold + 1.0))
-                    rec[k, here] = q - rate * pull
+                    rec[k, here] = q - scaled_rate(p, q, time_step) * pull
             return carry
 
         lax.fori_loop(0, MSTEPS, one_step, 0)
@@ -205,12 +244,13 @@
             target[1, k] = rec[k]
 
     first_slice = me * slots
-    last = slots - 1
+    unload(last)
     advance(it_ref.at[last], sent.at[0], first_slice + last)
     pl.semaphore_wait(barrier, chips + 1 + groups - 1)
     ring_one = remote(sent.at[0], relaxed.at[0], ring_s.at[0], ring_r.at[0], right)
     ring_one.start()
     for s in reversed(range(last)):
+        unload(s)
         advance(it_ref.at[s], relaxed.at[s + 1], first_slice + s)
     ring_two = remote(sent.at[1], previous.at[0], ring_s.at[1], ring_r.at[1], right)
     for s in reversed(range(slots)):
@@ -409,12 +449,6 @@
                 c_copy(k).wait_send()
 
 
-def pack(field):
-    rest = field[..., LANES:]
-    rest = jnp.concatenate([rest[..., 0, :, :], rest[..., 1, :, :]], axis=-1)
-    return jnp.concatenate([field[..., :LANES], rest[..., None, :, :]], axis=-3)
-
-
 def unpack(packed):
     rest = packed[..., 2, :, :]
     rest = jnp.stack([rest[..., : LANES // 2], rest[..., LANES // 2 :]], axis=-3)
@@ -426,28 +460,32 @@
     chips = 8
     groups = loop_size // (2 * chips)
     slots = iterate.shape[0]
-    conduct = jnp.zeros(labels.shape, jnp.float32)
-    for label_id, conduct_value in enumerate(conduct_table):
-        conduct = jnp.where(labels == label_id, jnp.float32(conduct_value), conduct)
-    state = pack(iterate)
     rows = labels.shape[1]
     tiles = rows // ROWS
     half = tiles // 2
     f32 = jnp.float32
+    state = (slots, 2, 3, rows, LANES)
     block = (3, ROWS, LANES)
     dma = pltpu.SemaphoreType.DMA
     out = pl.pallas_call(
         functools.partial(kernel, loop_size, chips, groups),
-        out_shape=jax.ShapeDtypeStruct(state.shape, f32),
-        in_specs=[pl.BlockSpec(memory_space=pltpu.VMEM)] * 3,
+        out_shape=jax.ShapeDtypeStruct(state, f32),
+        in_specs=[pl.BlockSpec(memory_space=pl.ANY)] * 3,
         out_specs=pl.BlockSpec(memory_space=pltpu.VMEM),
         scratch_shapes=[
+            pltpu.VMEM(iterate.shape, f32),
+            pltpu.VMEM(labels.shape, labels.dtype),
+            pltpu.VMEM(stim_mask.shape, stim_mask.dtype),
+            pltpu.VMEM(state, f32),
+            pltpu.VMEM((3, rows, LANES), f32),
+            pltpu.SemaphoreType.DMA((slots + 2,)),
             pltpu.VMEM((2, 3, rows + 2 * ROWS, LANES), f32),
+            pltpu.VMEM((3, rows, LANES), f32),
             pltpu.VMEM((3, rows, LANES), f32),
             pltpu.VMEM((1, 3, rows + 2 * ROWS, LANES), f32),
             pltpu.VMEM((6, 3, rows, LANES), f32),
-            pltpu.VMEM(state.shape, f32),
-            pltpu.VMEM(state.shape, f32),
+            pltpu.VMEM(state, f32),
+            pltpu.VMEM(state, f32),
             pltpu.VMEM((2, 2, 3, rows, LANES), f32),
             pltpu.VMEM((slots, tiles, 5) + block, f32),
             pltpu.VMEM((tiles, 5) + block, f32),
@@ -471,7 +509,7 @@
         compiler_params=pltpu.CompilerParams(
             collective_id=0, has_side_effects=True, vmem_limit_bytes=32 * 1024 * 1024
         ),
-    )(state, pack(conduct), pack(stim_mask.astype(f32)))
+    )(iterate, labels, stim_mask)
     return unpack(out)
 
 

time: 41.9 us -> 41.3 us (0.986)
  Pallas kernels: 35.6 us -> 37 us
  other arithmetic: 2.28 us -> 0.94 us
  local copies, waits for them, and re-layouts: 3.64 us -> 3.14 us
    slice x5 -> x0, local copies, waits for them, and re-layouts: 1.65 us -> none  [pack(): return jnp.concatenate([field[..., :LANES], rest[..., None, :, :]], axis=-3)]
    pallas_call x1, Pallas kernels: 35.6 us -> 37 us  [on_device(): pl.pallas_call(functools.partial(kernel, loop_size, chips, groups), out_s...]
    unnamed x6, local copies, waits for them, and re-layouts: 1.79 us -> 2.99 us
    select_n x1 -> x0, other arithmetic: 0.98 us -> none  [on_device(): conduct = jnp.where(labels == label_id, jnp.float32(conduct_value), conduct)]
where the time goes in v3:
time: 41.3 us; the launch traced here: 41.1 us
  Pallas kernels  37 us (90%)
  local copies, waits for them, and re-layouts  3.14 us (8%)
  other arithmetic  0.94 us (2%)
    pallas_call x1, Pallas kernels, on_device(): pl.pallas_call(functools.partial(kernel, loop_size, chips, groups), out_s...  37 us
    unnamed x6, local copies, waits for them, and re-layouts  2.99 us
    concatenate x1, other arithmetic, unpack(): return jnp.concatenate([packed[..., :2, :, :], rest], axis=-1)  0.94 us

profile of v3, /device:TPU:0, one launch (start us, length us, event | category | flops | bytes accessed | tf_op | source)
XLA Modules:
  0.0 41.1 jit_solution(1049337186935371959)
XLA Ops:
  0.0 0.0 copy-start
  0.0 1.1 %copy-done = f32[2,2,2,96,192]{4,3,2,1,0:T(8,128)S(1)} copy-done((f32[2,2,2,96,192]{4,3,2,1,0:T(8,128)S(1)}, f32[2,2,2,96,192]{4,3,2,1,0:T(8,128)}, u32[]{:S(2)}) %copy-start) | copy-done | bytes 589848
  1.1 0.0 copy-start.1
  1.1 0.9 %copy-done.1 = s32[2,96,192]{2,1,0:T(8,128)S(1)} copy-done((s32[2,96,192]{2,1,0:T(8,128)S(1)}, s32[2,96,192]{2,1,0:T(8,128)}, u32[]{:S(2)}) %copy-start.1) | copy-done | bytes 147480
  2.1 0.0 copy-start.2
  2.1 0.9 %copy-done.2 = s32[2,96,192]{2,1,0:T(8,128)S(1)} copy-done((s32[2,96,192]{2,1,0:T(8,128)S(1)}, s32[2,96,192]{2,1,0:T(8,128)}, u32[]{:S(2)}) %copy-start.2) | copy-done | bytes 147480
  3.0 37.0 %shard_map.37 = f32[2,2,3,96,128]{4,3,2,1,0:T(8,128)S(1)} custom-call(f32[2,2,2,96,192]{4,3,2,1,0:T(8,128)S(1)} %copy-done, s32[2,96,192]{2,1,0:T(8,128)S(1)} %copy-done.1, s32[2,96,192]{2,1,0:T(8,128)S(1)} %copy-done.2), custom_call_target="tpu_custom_call" | custom-call | tf_op jit(solution)/shard_map/pallas_call | solution.py:470
  40.0 0.1 slice_bitcast_fusion.1
  40.1 0.9 %pad_maximum_fusion = f32[2,2,2,96,192]{4,3,2,1,0:T(8,128)} fusion(f32[2,2,2,96,128]{4,3,2,1,0:T(8,128)S(1)} %slice.12, f32[2,2,1,96,64]{4,3,1,0,2:T(8,128)S(1)} %get-tuple-element.6, f32[2,2,1,96,64]{4,3,1,0,2:T(8,128)S(1)} %get-tuple-element.5), kind=kLoop, calls=%fused_computation | loop fusion | flops 196608 | bytes 1179648 | tf_op jit(solution)/shard_map/concatenate | solution.py:455
  (2 shorter events, 0.0 us)
Async XLA Ops:
  0.0 1.1 %copy-start = (f32[2,2,2,96,192]{4,3,2,1,0:T(8,128)S(1)}, f32[2,2,2,96,192]{4,3,2,1,0:T(8,128)}, u32[]{:S(2)}) copy-start(f32[2,2,2,96,192]{4,3,2,1,0:T(8,128)} %iterate_hbm.1) | copy-start | bytes 1769476
  1.1 0.9 %copy-start.1 = (s32[2,96,192]{2,1,0:T(8,128)S(1)}, s32[2,96,192]{2,1,0:T(8,128)}, u32[]{:S(2)}) copy-start(s32[2,96,192]{2,1,0:T(8,128)} %labels_hbm.1) | copy-start | bytes 442372
  2.1 0.9 %copy-start.2 = (s32[2,96,192]{2,1,0:T(8,128)S(1)}, s32[2,96,192]{2,1,0:T(8,128)}, u32[]{:S(2)}) copy-start(s32[2,96,192]{2,1,0:T(8,128)} %stim_hbm.1) | copy-start | bytes 442372

commit v4 on v3

--- a/solution.py
+++ b/solution.py
@@ -222,25 +222,25 @@
             rec[k] = source[1, k]
             drive[k] = switch * stim_ref[k]
 
-        def one_step(step, carry):
-            now = lax.rem(step, 2)
-            for t in range(tiles):
-                mid, up, down, left, right_, over = neighbours(pot, now, t, lane)
-                here = pl.ds(ROWS * t, ROWS)
-                for k in range(3):
-                    p, q = mid[k], rec[k, here]
-                    flow = coef[0, k, here] * up[k] + coef[1, k, here] * down[k]
-                    flow = flow + (coef[2, k, here] * left[k] + coef[3, k, here] * right_[k])
-                    flow = flow + (coef[4, k, here] * over[k] + drive[k, here])
-                    pull = q + excite_gain * (p * (p - (threshold + 1.0)))
-                    keep = coef[5, k, here] - time_step * pull
-                    pot[1 - now, k, pl.ds(ROWS + ROWS * t, ROWS)] = p * keep + flow
-                    rec[k, here] = q - scaled_rate(p, q, time_step) * pull
+        def two_steps(turn, carry):
+            for now in (0, 1):
+                for t in range(tiles):
+                    mid, up, down, left, right_, over = neighbours(pot, now, t, lane)
+                    here = pl.ds(ROWS * t, ROWS)
+                    for k in range(3):
+                        p, q = mid[k], rec[k, here]
+                        flow = coef[0, k, here] * up[k] + coef[1, k, here] * down[k]
+                        flow = flow + (coef[2, k, here] * left[k] + coef[3, k, here] * right_[k])
+                        flow = flow + (coef[4, k, here] * over[k] + drive[k, here])
+                        pull = q + excite_gain * (p * (p - (threshold + 1.0)))
+                        keep = coef[5, k, here] - time_step * pull
+                        pot[1 - now, k, pl.ds(ROWS + ROWS * t, ROWS)] = p * keep + flow
+                        rec[k, here] = q - scaled_rate(p, q, time_step) * pull
             return carry
 
-        lax.fori_loop(0, MSTEPS, one_step, 0)
-        for k in range(3):
-            target[0, k] = pot[MSTEPS % 2, k, pl.ds(ROWS, ROWS * tiles)]
+        lax.fori_loop(0, MSTEPS // 2, two_steps, 0)
+        for k in range(3):
+            target[0, k] = pot[0, k, pl.ds(ROWS, ROWS * tiles)]
             target[1, k] = rec[k]
 
     first_slice = me * slots

time: 41.3 us -> 41.6 us (level)
  no operation moved by 1% of the time
where the time goes in v4:
time: 41.6 us; the launch traced here: 41.4 us
  Pallas kernels  37.3 us (90%)
  local copies, waits for them, and re-layouts  3.14 us (8%)
  other arithmetic  0.94 us (2%)
    pallas_call x1, Pallas kernels, on_device(): pl.pallas_call(functools.partial(kernel, loop_size, chips, groups), out_s...  37.3 us
    unnamed x6, local copies, waits for them, and re-layouts  2.99 us
    concatenate x1, other arithmetic, unpack(): return jnp.concatenate([packed[..., :2, :, :], rest], axis=-1)  0.94 us

profile of v4, /device:TPU:0, one launch (start us, length us, event | category | flops | bytes accessed | tf_op | source)
XLA Modules:
  0.0 41.4 jit_solution(14110560755206697162)
XLA Ops:
  0.0 0.0 copy-start
  0.0 1.1 %copy-done = f32[2,2,2,96,192]{4,3,2,1,0:T(8,128)S(1)} copy-done((f32[2,2,2,96,192]{4,3,2,1,0:T(8,128)S(1)}, f32[2,2,2,96,192]{4,3,2,1,0:T(8,128)}, u32[]{:S(2)}) %copy-start) | copy-done | bytes 589848
  1.1 0.0 copy-start.1
  1.1 0.9 %copy-done.1 = s32[2,96,192]{2,1,0:T(8,128)S(1)} copy-done((s32[2,96,192]{2,1,0:T(8,128)S(1)}, s32[2,96,192]{2,1,0:T(8,128)}, u32[]{:S(2)}) %copy-start.1) | copy-done | bytes 147480
  2.1 0.0 copy-start.2
  2.1 0.9 %copy-done.2 = s32[2,96,192]{2,1,0:T(8,128)S(1)} copy-done((s32[2,96,192]{2,1,0:T(8,128)S(1)}, s32[2,96,192]{2,1,0:T(8,128)}, u32[]{:S(2)}) %copy-start.2) | copy-done | bytes 147480
  3.0 37.3 %shard_map.37 = f32[2,2,3,96,128]{4,3,2,1,0:T(8,128)S(1)} custom-call(f32[2,2,2,96,192]{4,3,2,1,0:T(8,128)S(1)} %copy-done, s32[2,96,192]{2,1,0:T(8,128)S(1)} %copy-done.1, s32[2,96,192]{2,1,0:T(8,128)S(1)} %copy-done.2), custom_call_target="tpu_custom_call" | custom-call | tf_op jit(solution)/shard_map/pallas_call | solution.py:470
  40.4 0.1 slice_bitcast_fusion.1
  40.5 0.9 %pad_maximum_fusion = f32[2,2,2,96,192]{4,3,2,1,0:T(8,128)} fusion(f32[2,2,2,96,128]{4,3,2,1,0:T(8,128)S(1)} %slice.12, f32[2,2,1,96,64]{4,3,1,0,2:T(8,128)S(1)} %get-tuple-element.6, f32[2,2,1,96,64]{4,3,1,0,2:T(8,128)S(1)} %get-tuple-element.5), kind=kLoop, calls=%fused_computation | loop fusion | flops 196608 | bytes 1179648 | tf_op jit(solution)/shard_map/concatenate | solution.py:455
  (2 shorter events, 0.0 us)
Async XLA Ops:
  0.0 1.1 %copy-start = (f32[2,2,2,96,192]{4,3,2,1,0:T(8,128)S(1)}, f32[2,2,2,96,192]{4,3,2,1,0:T(8,128)}, u32[]{:S(2)}) copy-start(f32[2,2,2,96,192]{4,3,2,1,0:T(8,128)} %iterate_hbm.1) | copy-start | bytes 1769476
  1.1 0.9 %copy-start.1 = (s32[2,96,192]{2,1,0:T(8,128)S(1)}, s32[2,96,192]{2,1,0:T(8,128)}, u32[]{:S(2)}) copy-start(s32[2,96,192]{2,1,0:T(8,128)} %labels_hbm.1) | copy-start | bytes 442372
  2.1 0.9 %copy-start.2 = (s32[2,96,192]{2,1,0:T(8,128)S(1)}, s32[2,96,192]{2,1,0:T(8,128)}, u32[]{:S(2)}) copy-start(s32[2,96,192]{2,1,0:T(8,128)} %stim_hbm.1) | copy-start | bytes 442372

commit v5 on v4

--- a/solution.py
+++ b/solution.py
@@ -252,16 +252,28 @@
     for s in reversed(range(last)):
         unload(s)
         advance(it_ref.at[s], relaxed.at[s + 1], first_slice + s)
-    ring_two = remote(sent.at[1], previous.at[0], ring_s.at[1], ring_r.at[1], right)
+
+    def ring_two(t):
+        here = pl.ds(pl.multiple_of(ROWS * t, ROWS), ROWS)
+        return remote(
+            sent.at[1, :, :, here], previous.at[0, :, :, here],
+            ring_s.at[1 + t], ring_r.at[1 + t], right,
+        )
+
+    def send_two(turn, carry):
+        j = lax.rem(turn + lax.rem(right // 2, chips), half)
+        ring_two(half * core + j).start()
+        ring_two(half * (1 - core) + j).start()
+        return carry
+
     for s in reversed(range(slots)):
         if s == 0:
             ring_one.wait_recv()
         if s == last:
             advance(relaxed.at[s], sent.at[1], first_slice + s)
-            ring_two.start()
+            lax.fori_loop(0, half, send_two, 0)
         else:
             advance(relaxed.at[s], previous.at[s + 1], first_slice + s)
-    ring_two.wait_recv()
 
     def make_maps(t):
         here = pl.ds(pl.multiple_of(ROWS * t, ROWS), ROWS)
@@ -286,18 +298,6 @@
             own.at[half * (1 - core) + j], got.at[j], a_s.at[j], a_r.at[j], partner
         )
 
-    def phase_send(j, carry):
-        make_maps(half * (1 - core) + j)
-        a_copy(j).start()
-        return carry
-
-    def phase_keep(j, carry):
-        make_maps(half * core + j)
-        return carry
-
-    lax.fori_loop(0, half, phase_send, 0)
-    lax.fori_loop(0, half, phase_keep, 0)
-
     def owner_of(j):
         return j + (j + half - 1) // half + (j + 1) // half
 
@@ -307,7 +307,7 @@
             base + 2 * owner_of(j) + core,
         )
 
-    def phase_pair(turn, carry):
+    def pair_step(turn):
         j = lax.rem(turn + chip, half)
         a_copy(j).wait_recv()
         for k in range(3):
@@ -329,9 +329,23 @@
         def _():
             parts[chip] = pair[j]
 
+    def phase_maps(turn, carry):
+        j = lax.rem(turn + chip, half)
+        away, mine = half * (1 - core) + j, half * core + j
+        ring_two(away).wait_recv()
+        make_maps(away)
+        a_copy(j).start()
+        ring_two(mine).wait_recv()
+        make_maps(mine)
+
+        @pl.when(turn > 0)
+        def _():
+            pair_step(turn - 1)
+
         return carry
 
-    lax.fori_loop(0, half, phase_pair, 0)
+    lax.fori_loop(0, half, phase_maps, 0)
+    pair_step(half - 1)
 
     def c_copy(k):
         return remote(
@@ -432,7 +446,8 @@
     lax.fori_loop(0, half, phase_theirs, 0)
 
     ring_one.wait_send()
-    ring_two.wait_send()
+    for t in range(tiles):
+        ring_two(t).wait_send()
     for j in range(half):
         a_copy(j).wait_send()
         d_copy(j).wait_send()
@@ -499,7 +514,7 @@
             pltpu.VMEM((half, 2) + block, f32),
             pltpu.VMEM((half, 2) + block, f32),
             pltpu.VMEM((tiles, 2) + block, f32),
-            dma((2,)), dma((2,)),
+            dma((1 + tiles,)), dma((1 + tiles,)),
             dma((half,)), dma((half,)),
             dma((half,)), dma((chips,)),
             dma((groups,)), dma((groups,)),

time: 41.6 us -> 39.1 us (0.940)
  Pallas kernels: 37.3 us -> 34.8 us
    pallas_call x1, Pallas kernels: 37.3 us -> 34.8 us  [on_device(): pl.pallas_call(functools.partial(kernel, loop_size, chips, groups), out_s...]
where the time goes in v5:
time: 39.1 us; the launch traced here: 38.9 us
  Pallas kernels  34.8 us (89%)
  local copies, waits for them, and re-layouts  3.14 us (8%)
  other arithmetic  0.94 us (2%)
    pallas_call x1, Pallas kernels, on_device(): pl.pallas_call(functools.partial(kernel, loop_size, chips, groups), out_s...  34.8 us
    unnamed x6, local copies, waits for them, and re-layouts  2.99 us
    concatenate x1, other arithmetic, unpack(): return jnp.concatenate([packed[..., :2, :, :], rest], axis=-1)  0.94 us

profile of v5, /device:TPU:0, one launch (start us, length us, event | category | flops | bytes accessed | tf_op | source)
XLA Modules:
  0.0 38.9 jit_solution(5578865766517040388)
XLA Ops:
  0.0 0.0 copy-start
  0.0 1.1 %copy-done = f32[2,2,2,96,192]{4,3,2,1,0:T(8,128)S(1)} copy-done((f32[2,2,2,96,192]{4,3,2,1,0:T(8,128)S(1)}, f32[2,2,2,96,192]{4,3,2,1,0:T(8,128)}, u32[]{:S(2)}) %copy-start) | copy-done | bytes 589848
  1.1 0.0 copy-start.1
  1.1 0.9 %copy-done.1 = s32[2,96,192]{2,1,0:T(8,128)S(1)} copy-done((s32[2,96,192]{2,1,0:T(8,128)S(1)}, s32[2,96,192]{2,1,0:T(8,128)}, u32[]{:S(2)}) %copy-start.1) | copy-done | bytes 147480
  2.1 0.0 copy-start.2
  2.1 0.9 %copy-done.2 = s32[2,96,192]{2,1,0:T(8,128)S(1)} copy-done((s32[2,96,192]{2,1,0:T(8,128)S(1)}, s32[2,96,192]{2,1,0:T(8,128)}, u32[]{:S(2)}) %copy-start.2) | copy-done | bytes 147480
  3.0 34.8 %shard_map.37 = f32[2,2,3,96,128]{4,3,2,1,0:T(8,128)S(1)} custom-call(f32[2,2,2,96,192]{4,3,2,1,0:T(8,128)S(1)} %copy-done, s32[2,96,192]{2,1,0:T(8,128)S(1)} %copy-done.1, s32[2,96,192]{2,1,0:T(8,128)S(1)} %copy-done.2), custom_call_target="tpu_custom_call" | custom-call | tf_op jit(solution)/shard_map/pallas_call | solution.py:485
  37.8 0.1 slice_bitcast_fusion.1
  38.0 0.9 %pad_maximum_fusion = f32[2,2,2,96,192]{4,3,2,1,0:T(8,128)} fusion(f32[2,2,2,96,128]{4,3,2,1,0:T(8,128)S(1)} %slice.12, f32[2,2,1,96,64]{4,3,1,0,2:T(8,128)S(1)} %get-tuple-element.6, f32[2,2,1,96,64]{4,3,1,0,2:T(8,128)S(1)} %get-tuple-element.5), kind=kLoop, calls=%fused_computation | loop fusion | flops 196608 | bytes 1179648 | tf_op jit(solution)/shard_map/concatenate | solution.py:470
  (2 shorter events, 0.0 us)
Async XLA Ops:
  0.0 1.1 %copy-start = (f32[2,2,2,96,192]{4,3,2,1,0:T(8,128)S(1)}, f32[2,2,2,96,192]{4,3,2,1,0:T(8,128)}, u32[]{:S(2)}) copy-start(f32[2,2,2,96,192]{4,3,2,1,0:T(8,128)} %iterate_hbm.1) | copy-start | bytes 1769476
  1.1 0.9 %copy-start.1 = (s32[2,96,192]{2,1,0:T(8,128)S(1)}, s32[2,96,192]{2,1,0:T(8,128)}, u32[]{:S(2)}) copy-start(s32[2,96,192]{2,1,0:T(8,128)} %labels_hbm.1) | copy-start | bytes 442372
  2.1 0.9 %copy-start.2 = (s32[2,96,192]{2,1,0:T(8,128)S(1)}, s32[2,96,192]{2,1,0:T(8,128)}, u32[]{:S(2)}) copy-start(s32[2,96,192]{2,1,0:T(8,128)} %stim_hbm.1) | copy-start | bytes 442372

commit v6 on v5

--- a/solution.py
+++ b/solution.py
@@ -129,8 +129,6 @@
     ]
     for s in reversed(range(slots)):
         loads.append(pltpu.make_async_copy(iterate_hbm.at[s], raw.at[s], load_sem.at[s]))
-    for load in loads:
-        load.start()
     half = tiles // 2
     me = lax.axis_index("tm")
     core = lax.rem(me, 2)
@@ -162,6 +160,9 @@
             src_ref=source, dst_ref=target, send_sem=send_sem, recv_sem=recv_sem,
             device_id={"tm": device}, device_id_type=pl.DeviceIdType.MESH,
         )
+
+    for load in loads:
+        load.start()
 
     lane = lax.broadcasted_iota(jnp.int32, (ROWS, LANES), 1)
     row = lax.broadcasted_iota(jnp.int32, (ROWS, LANES), 0)
@@ -427,13 +428,10 @@
                 entry[half * core + j, n, k] = jnp.where(core == 0, zero[n], one[n])
                 pass_on[j, n, k] = jnp.where(core == 0, one[n], zero[n])
         d_copy(j).start()
-        return carry
-
-    lax.fori_loop(0, half, phase_back, 0)
-
-    def phase_mine(j, carry):
         finish(half * core + j)
         return carry
+
+    lax.fori_loop(0, half, phase_back, 0)
 
     def phase_theirs(j, carry):
         remote(
@@ -442,7 +440,6 @@
         finish(half * (1 - core) + j)
         return carry
 
-    lax.fori_loop(0, half, phase_mine, 0)
     lax.fori_loop(0, half, phase_theirs, 0)
 
     ring_one.wait_send()

time: 39.1 us -> 39 us (level)
  no operation moved by 1% of the time
where the time goes in v6:
time: 39 us; the launch traced here: 38.8 us
  Pallas kernels  34.7 us (89%)
  local copies, waits for them, and re-layouts  3.14 us (8%)
  other arithmetic  0.94 us (2%)
    pallas_call x1, Pallas kernels, on_device(): pl.pallas_call(functools.partial(kernel, loop_size, chips, groups), out_s...  34.7 us
    unnamed x6, local copies, waits for them, and re-layouts  2.99 us
    concatenate x1, other arithmetic, unpack(): return jnp.concatenate([packed[..., :2, :, :], rest], axis=-1)  0.94 us

profile of v6, /device:TPU:0, one launch (start us, length us, event | category | flops | bytes accessed | tf_op | source)
XLA Modules:
  0.0 38.8 jit_solution(10754845952644715775)
XLA Ops:
  0.0 0.0 copy-start
  0.0 1.1 %copy-done = f32[2,2,2,96,192]{4,3,2,1,0:T(8,128)S(1)} copy-done((f32[2,2,2,96,192]{4,3,2,1,0:T(8,128)S(1)}, f32[2,2,2,96,192]{4,3,2,1,0:T(8,128)}, u32[]{:S(2)}) %copy-start) | copy-done | bytes 589848
  1.1 0.0 copy-start.1
  1.1 0.9 %copy-done.1 = s32[2,96,192]{2,1,0:T(8,128)S(1)} copy-done((s32[2,96,192]{2,1,0:T(8,128)S(1)}, s32[2,96,192]{2,1,0:T(8,128)}, u32[]{:S(2)}) %copy-start.1) | copy-done | bytes 147480
  2.1 0.0 copy-start.2
  2.1 0.9 %copy-done.2 = s32[2,96,192]{2,1,0:T(8,128)S(1)} copy-done((s32[2,96,192]{2,1,0:T(8,128)S(1)}, s32[2,96,192]{2,1,0:T(8,128)}, u32[]{:S(2)}) %copy-start.2) | copy-done | bytes 147480
  3.0 34.7 %shard_map.37 = f32[2,2,3,96,128]{4,3,2,1,0:T(8,128)S(1)} custom-call(f32[2,2,2,96,192]{4,3,2,1,0:T(8,128)S(1)} %copy-done, s32[2,96,192]{2,1,0:T(8,128)S(1)} %copy-done.1, s32[2,96,192]{2,1,0:T(8,128)S(1)} %copy-done.2), custom_call_target="tpu_custom_call" | custom-call | tf_op jit(solution)/shard_map/pallas_call | solution.py:482
  37.8 0.1 slice_bitcast_fusion.1
  37.9 0.9 %pad_maximum_fusion = f32[2,2,2,96,192]{4,3,2,1,0:T(8,128)} fusion(f32[2,2,2,96,128]{4,3,2,1,0:T(8,128)S(1)} %slice.12, f32[2,2,1,96,64]{4,3,1,0,2:T(8,128)S(1)} %get-tuple-element.6, f32[2,2,1,96,64]{4,3,1,0,2:T(8,128)S(1)} %get-tuple-element.5), kind=kLoop, calls=%fused_computation | loop fusion | flops 196608 | bytes 1179648 | tf_op jit(solution)/shard_map/concatenate | solution.py:467
  (2 shorter events, 0.0 us)
Async XLA Ops:
  0.0 1.1 %copy-start = (f32[2,2,2,96,192]{4,3,2,1,0:T(8,128)S(1)}, f32[2,2,2,96,192]{4,3,2,1,0:T(8,128)}, u32[]{:S(2)}) copy-start(f32[2,2,2,96,192]{4,3,2,1,0:T(8,128)} %iterate_hbm.1) | copy-start | bytes 1769476
  1.1 0.9 %copy-start.1 = (s32[2,96,192]{2,1,0:T(8,128)S(1)}, s32[2,96,192]{2,1,0:T(8,128)}, u32[]{:S(2)}) copy-start(s32[2,96,192]{2,1,0:T(8,128)} %labels_hbm.1) | copy-start | bytes 442372
  2.1 0.9 %copy-start.2 = (s32[2,96,192]{2,1,0:T(8,128)S(1)}, s32[2,96,192]{2,1,0:T(8,128)}, u32[]{:S(2)}) copy-start(s32[2,96,192]{2,1,0:T(8,128)} %stim_hbm.1) | copy-start | bytes 442372

commit v7 on v6

--- a/solution.py
+++ b/solution.py
@@ -248,8 +248,15 @@
     unload(last)
     advance(it_ref.at[last], sent.at[0], first_slice + last)
     pl.semaphore_wait(barrier, chips + 1 + groups - 1)
-    ring_one = remote(sent.at[0], relaxed.at[0], ring_s.at[0], ring_r.at[0], right)
-    ring_one.start()
+    ring_one = [
+        remote(
+            sent.at[0, n], relaxed.at[0, n], ring_s.at[n * (1 + tiles)],
+            ring_r.at[n * (1 + tiles)], right,
+        )
+        for n in range(2)
+    ]
+    for copy in ring_one:
+        copy.start()
     for s in reversed(range(last)):
         unload(s)
         advance(it_ref.at[s], relaxed.at[s + 1], first_slice + s)
@@ -269,7 +276,8 @@
 
     for s in reversed(range(slots)):
         if s == 0:
-            ring_one.wait_recv()
+            for copy in ring_one:
+                copy.wait_recv()
         if s == last:
             advance(relaxed.at[s], sent.at[1], first_slice + s)
             lax.fori_loop(0, half, send_two, 0)
@@ -442,7 +450,8 @@
 
     lax.fori_loop(0, half, phase_theirs, 0)
 
-    ring_one.wait_send()
+    for copy in ring_one:
+        copy.wait_send()
     for t in range(tiles):
         ring_two(t).wait_send()
     for j in range(half):
@@ -511,7 +520,7 @@
             pltpu.VMEM((half, 2) + block, f32),
             pltpu.VMEM((half, 2) + block, f32),
             pltpu.VMEM((tiles, 2) + block, f32),
-            dma((1 + tiles,)), dma((1 + tiles,)),
+            dma((2 + tiles,)), dma((2 + tiles,)),
             dma((half,)), dma((half,)),
             dma((half,)), dma((chips,)),
             dma((groups,)), dma((groups,)),

time: 39 us -> 39 us (level)
  no operation moved by 1% of the time
where the time goes in v7:
time: 39 us; the launch traced here: 38.8 us
  Pallas kernels  34.7 us (89%)
  local copies, waits for them, and re-layouts  3.14 us (8%)
  other arithmetic  0.94 us (2%)
    pallas_call x1, Pallas kernels, on_device(): pl.pallas_call(functools.partial(kernel, loop_size, chips, groups), out_s...  34.7 us
    unnamed x6, local copies, waits for them, and re-layouts  2.99 us
    concatenate x1, other arithmetic, unpack(): return jnp.concatenate([packed[..., :2, :, :], rest], axis=-1)  0.94 us

profile of v7, /device:TPU:0, one launch (start us, length us, event | category | flops | bytes accessed | tf_op | source)
XLA Modules:
  0.0 38.8 jit_solution(17163217618251630071)
XLA Ops:
  0.0 0.0 copy-start
  0.0 1.1 %copy-done = f32[2,2,2,96,192]{4,3,2,1,0:T(8,128)S(1)} copy-done((f32[2,2,2,96,192]{4,3,2,1,0:T(8,128)S(1)}, f32[2,2,2,96,192]{4,3,2,1,0:T(8,128)}, u32[]{:S(2)}) %copy-start) | copy-done | bytes 589848
  1.1 0.0 copy-start.1
  1.1 0.9 %copy-done.1 = s32[2,96,192]{2,1,0:T(8,128)S(1)} copy-done((s32[2,96,192]{2,1,0:T(8,128)S(1)}, s32[2,96,192]{2,1,0:T(8,128)}, u32[]{:S(2)}) %copy-start.1) | copy-done | bytes 147480
  2.1 0.0 copy-start.2
  2.1 0.9 %copy-done.2 = s32[2,96,192]{2,1,0:T(8,128)S(1)} copy-done((s32[2,96,192]{2,1,0:T(8,128)S(1)}, s32[2,96,192]{2,1,0:T(8,128)}, u32[]{:S(2)}) %copy-start.2) | copy-done | bytes 147480
  3.0 34.7 %shard_map.37 = f32[2,2,3,96,128]{4,3,2,1,0:T(8,128)S(1)} custom-call(f32[2,2,2,96,192]{4,3,2,1,0:T(8,128)S(1)} %copy-done, s32[2,96,192]{2,1,0:T(8,128)S(1)} %copy-done.1, s32[2,96,192]{2,1,0:T(8,128)S(1)} %copy-done.2), custom_call_target="tpu_custom_call" | custom-call | tf_op jit(solution)/shard_map/pallas_call | solution.py:491
  37.8 0.1 slice_bitcast_fusion.1
  37.9 0.9 %pad_maximum_fusion = f32[2,2,2,96,192]{4,3,2,1,0:T(8,128)} fusion(f32[2,2,2,96,128]{4,3,2,1,0:T(8,128)S(1)} %slice.12, f32[2,2,1,96,64]{4,3,1,0,2:T(8,128)S(1)} %get-tuple-element.6, f32[2,2,1,96,64]{4,3,1,0,2:T(8,128)S(1)} %get-tuple-element.5), kind=kLoop, calls=%fused_computation | loop fusion | flops 196608 | bytes 1179648 | tf_op jit(solution)/shard_map/concatenate | solution.py:476
  (2 shorter events, 0.0 us)
Async XLA Ops:
  0.0 1.1 %copy-start = (f32[2,2,2,96,192]{4,3,2,1,0:T(8,128)S(1)}, f32[2,2,2,96,192]{4,3,2,1,0:T(8,128)}, u32[]{:S(2)}) copy-start(f32[2,2,2,96,192]{4,3,2,1,0:T(8,128)} %iterate_hbm.1) | copy-start | bytes 1769476
  1.1 0.9 %copy-start.1 = (s32[2,96,192]{2,1,0:T(8,128)S(1)}, s32[2,96,192]{2,1,0:T(8,128)}, u32[]{:S(2)}) copy-start(s32[2,96,192]{2,1,0:T(8,128)} %labels_hbm.1) | copy-start | bytes 442372
  2.1 0.9 %copy-start.2 = (s32[2,96,192]{2,1,0:T(8,128)S(1)}, s32[2,96,192]{2,1,0:T(8,128)}, u32[]{:S(2)}) copy-start(s32[2,96,192]{2,1,0:T(8,128)} %stim_hbm.1) | copy-start | bytes 442372
